TPU v7x, 512 devices: a whole 4x4x16 slice. The times are simulated.
512 devices in a mesh: dom: 32 (over x, y, core), cls: 16 (over z).
Axes of the slice: x: 4, y: 4, z: 16, core: 2. Of those that a mesh axis runs over, the one named last changes fastest.
Arguments:
- images: bfloat16 [16384, 128, 128], P(('dom', 'cls')), may hold values from -6 to 6
- class_ids: int32 [16384], P(('dom', 'cls')), may hold values from 0 to 255, as said below
- shifts: int32 [16384, 2], P(('dom', 'cls')), may hold values from -16 to 16
- defocus_bins: int32 [16384], P(('dom', 'cls')), may hold values from 0 to 31
- defocus: float32 [32], replicated, may hold values from 20 to 200
- regular: float32 [128, 128], replicated, may hold values from 1 to 32
Outputs:
- class_avg: float32 [256, 128, 128], P('cls')
Inputs may be any that keep to these rules, and one draw needn't show every extreme that they name: `class_ids`: the owner of class k is k // 16. Among the 32 particles of one device exactly 8 have classes of one owner, and every other owner has at most 2 of them, exactly 2 for some; all devices with the same dom index have that same most loaded owner.
All inputs are finite; a program needn't handle non-finite values.
Results may differ from a plain program's by a relative error of at most 0.0055.
Values may be sent and summed in bfloat16 or wider, within the bound.
No kernel may reach another device: no remote copies, remote signals or barrier semaphores. Data moves between devices by JAX's collectives and lax.ppermute only.
A program may use at most 64 MiB of HBM per device.

v0:
```python
import math

import jax
import jax.numpy as jnp
from jax import lax
from jax.sharding import PartitionSpec as P

OWNED = 16


PHASE = 0.1
EPSILON = 1e-05


def hartley_tables(image_side):
    indices = jnp.arange(image_side, dtype=jnp.int32)
    product = indices[:, None] * indices[None, :] % image_side
    angles = product.astype(jnp.float32) * (2.0 * math.pi / image_side)
    return (jnp.cos(angles), jnp.sin(angles))


def frequency_squared(image_side):
    indices = jnp.arange(image_side, dtype=jnp.int32)
    signed = (
        jnp.where(indices < image_side // 2, indices, indices - image_side).astype(jnp.float32)
        / image_side
    )
    return signed[:, None] * signed[:, None] + signed[None, :] * signed[None, :]


def lookup(bins, defocus):
    levels = jnp.arange(defocus.shape[0], dtype=jnp.int32)
    return jnp.sum(jnp.where(bins[:, None] == levels[None, :], defocus[None, :], 0.0), axis=1)


def weigh(pictures, offsets, bins, defocus):
    count_rows = pictures.shape[0]
    image_side = pictures.shape[1]
    indices = jnp.arange(image_side, dtype=jnp.int32)
    source_rows = (indices[None, :] - offsets[:, 0:1]) % image_side
    source_cols = (indices[None, :] - offsets[:, 1:2]) % image_side
    row_select = (source_rows[:, :, None] == indices[None, None, :]).astype(jnp.bfloat16)
    col_select = (source_cols[:, :, None] == indices[None, None, :]).astype(jnp.bfloat16)
    shifted = jnp.einsum(
        "pij,pjk->pik", row_select, pictures, preferred_element_type=jnp.float32
    ).astype(jnp.bfloat16)
    shifted = jnp.einsum(
        "pik,plk->pil", shifted, col_select, preferred_element_type=jnp.float32
    ).astype(jnp.bfloat16)
    cosine, sine_table = hartley_tables(image_side)
    factor = 1.0 / math.sqrt(image_side)
    right_table = (
        jnp.concatenate([cosine + sine_table, cosine - sine_table], axis=1) * factor
    ).astype(jnp.bfloat16)
    left_table = (jnp.stack([cosine, sine_table]) * factor).astype(jnp.bfloat16)
    halves = jnp.dot(
        shifted.reshape(count_rows * image_side, image_side),
        right_table,
        preferred_element_type=jnp.float32,
    ).astype(jnp.bfloat16)
    halves = halves.reshape(count_rows, image_side, 2, image_side)
    spectrum = jnp.einsum("kux,pxkv->puv", left_table, halves, preferred_element_type=jnp.float32)
    ctf_values = -jnp.sin(
        lookup(bins, defocus)[:, None, None] * frequency_squared(image_side)[None] + PHASE
    )
    return (ctf_values * spectrum).astype(jnp.bfloat16).reshape(count_rows, image_side * image_side)


def body(images, class_ids, shifts, defocus_bins, defocus, regular):
    owners = lax.axis_size("cls")
    count_local = images.shape[0]
    image_side = images.shape[1]
    pixels = image_side * image_side
    capacity = min(4 * count_local // owners, count_local // 2)
    owner_of = class_ids // OWNED
    local_class = class_ids % OWNED
    member = (owner_of[:, None] == jnp.arange(owners, dtype=jnp.int32)[None, :]).astype(jnp.int32)
    before = jnp.cumsum(member, axis=0) - member
    ranked = jnp.sum(before * member, axis=1)
    slot_width = (count_local - capacity + owners - 2) // (owners - 1)
    slot_count = owners * slot_width
    target = jnp.where(ranked < slot_width, owner_of * slot_width + ranked, -1)
    matches = jnp.arange(slot_count, dtype=jnp.int32)[:, None] == target[None, :]
    filled = jnp.any(matches, axis=1)
    dispatch = matches.astype(jnp.bfloat16)

    def select_ints(selection, values):
        return jnp.sum(jnp.where(selection, values[None, :], 0), axis=1)

    slot_class = jnp.where(filled, select_ints(matches, local_class), OWNED)
    slot_bin = select_ints(matches, defocus_bins)
    payload = weigh(images, shifts, defocus_bins, defocus)
    outgoing = jnp.dot(dispatch, payload, preferred_element_type=jnp.float32).astype(jnp.bfloat16)
    outgoing = outgoing.reshape(owners, slot_width, pixels)
    labels = jnp.stack([slot_class, slot_bin], axis=1).reshape(owners, slot_width, 2)
    arrived, arrived_labels = (
        lax.all_to_all(outgoing, "cls", split_axis=0, concat_axis=0, tiled=True),
        lax.all_to_all(labels, "cls", split_axis=0, concat_axis=0, tiled=True),
    )
    arrived_rows = arrived.reshape(slot_count, pixels)
    arrived_tags = arrived_labels.reshape(slot_count, 2)
    surplus = capacity - slot_width
    extra_matches = (
        jnp.arange(surplus, dtype=jnp.int32)[:, None]
        == jnp.where(ranked >= slot_width, ranked - slot_width, -1)[None, :]
    )
    extra_filled = jnp.any(extra_matches, axis=1)
    extra_rows = jnp.dot(
        extra_matches.astype(jnp.bfloat16), payload, preferred_element_type=jnp.float32
    ).astype(jnp.bfloat16)
    extra_tags = jnp.stack(
        [
            select_ints(extra_matches, local_class),
            select_ints(extra_matches, defocus_bins),
            select_ints(extra_matches, shifts[:, 0]),
            select_ints(extra_matches, shifts[:, 1]),
            jnp.where(extra_filled, select_ints(extra_matches, owner_of), -1),
        ],
        axis=1,
    )
    gathered_rows, gathered_tags = (
        lax.all_gather(extra_rows, "cls", axis=0, tiled=True),
        lax.all_gather(extra_tags, "cls", axis=0, tiled=True),
    )
    mine = gathered_tags[:, 4] == lax.axis_index("cls")
    kept_class = jnp.where(mine, gathered_tags[:, 0], OWNED)
    arrived_rows = jnp.concatenate([arrived_rows, gathered_rows], axis=0)
    arrived_tags = jnp.concatenate(
        [arrived_tags, jnp.stack([kept_class, gathered_tags[:, 1]], axis=1)], axis=0
    )
    bin_count = defocus.shape[0]
    class_select = (jnp.arange(OWNED, dtype=jnp.int32)[:, None] == arrived_tags[None, :, 0]).astype(
        jnp.bfloat16
    )
    bin_select = (arrived_tags[:, 1:2] == jnp.arange(bin_count, dtype=jnp.int32)[None, :]).astype(
        jnp.bfloat16
    )
    numerator = jnp.dot(class_select, arrived_rows, preferred_element_type=jnp.float32)
    counts = jnp.dot(class_select, bin_select, preferred_element_type=jnp.float32)
    squared = frequency_squared(image_side).reshape(pixels)
    ctf_table = jnp.sin(defocus[:, None] * squared[None, :] + PHASE)
    ctf_table = ctf_table * ctf_table
    denominator = jnp.dot(counts, ctf_table, precision=lax.Precision.HIGHEST)
    numerator, denominator = lax.psum((numerator, denominator), "dom")
    average = numerator / (denominator + regular.reshape(1, pixels))
    cosine, sine_table = hartley_tables(image_side)
    right_table = jnp.concatenate([cosine + sine_table, cosine - sine_table], axis=1)
    left_table = jnp.stack([cosine, sine_table])
    halves = jnp.dot(
        average.reshape(OWNED * image_side, image_side),
        right_table,
        precision=lax.Precision.HIGHEST,
    )
    halves = halves.reshape(OWNED, image_side, 2, image_side)
    real_image = jnp.einsum("kux,pxkv->puv", left_table, halves, precision=lax.Precision.HIGHEST)
    power_mean = jnp.mean(real_image * real_image, axis=(1, 2), keepdims=True)
    return real_image / jnp.sqrt(power_mean + EPSILON)


def solution(mesh):
    in_specs = (
        P(("dom", "cls"), None, None),
        P(("dom", "cls")),
        P(("dom", "cls"), None),
        P(("dom", "cls")),
        P(),
        P(),
    )
    out_specs = P("cls", None, None)
    return jax.shard_map(body, mesh=mesh, in_specs=in_specs, out_specs=out_specs, check_vma=False)
```

profile of v0, /device:TPU:1, one launch (start us, length us, event | category | flops | bytes accessed | tf_op | source)
XLA Modules:
  0.0 312.0 jit_solution(7579158338892761363)
XLA Ops:
  7.1 0.7 and_select_fusion
  8.1 0.8 slice_bitcast_fusion.3
  9.0 2.4 fusion.15
  11.4 1.9 convolution_convert_fusion.2
  13.4 2.1 reshape.289
  15.8 9.2 %fusion.5 = bf16[32,128,128]{1,2,0:T(8,128)(2,1)S(1)} fusion(bf16[32,128,2,128]{3,2,1,0:T(2,128)(2,1)} %reshape.289, f32[128,128]{0,1:T(8,128)S(1)} %copy.34, f32[32]{0:T(128)S(1)} %select_reduce_fusion, f32[1,128,128]{2,1,0:T(8,128)S(1)} %get-tuple-element.32, f32[1,128,128]{2,1,0:T(8,128)S(1)} %get-tuple-element.33), kind=kOutput, calls=%fused_computation.9 | convolution fusion | flops 271155200 | bytes 3342464 | tf_op jit(solution)/shard_map/kux,pxkv->puv/dot_general | solution.py:62
  25.0 0.7 copy.36
  25.7 1.4 fusion
  27.5 0.6 copy.30
  28.1 15.7 %all-to-all-start = ((s32[16,2,2]{1,2,0:T(2,128)}), s32[16,2,2]{1,2,0:T(2,128)S(1)}, u32[]{:S(2)}, u32[]{:S(2)}) async-start(s32[16,2,2]{1,2,0:T(2,128)} %copy.30), calls=%async_computation | async-start | bytes 32768 | tf_op jit(solution)/shard_map/all_to_all | solution.py:98
  43.9 0.7 convolution_convert_fusion
  44.6 1.5 reshape.291
  46.1 9.2 %all-to-all-done = s32[16,2,2]{1,2,0:T(2,128)S(1)} async-done(((s32[16,2,2]{1,2,0:T(2,128)}), s32[16,2,2]{1,2,0:T(2,128)S(1)}, u32[]{:S(2)}, u32[]{:S(2)}) %all-to-all-start) | async-done | bytes 288 | tf_op jit(solution)/shard_map/all_to_all | solution.py:98
  55.3 3.7 %all-to-all-start.1 = ((bf16[16,2,16384]{2,1,0:T(2,128)(2,1)}), bf16[16,2,16384]{2,1,0:T(2,128)(2,1)S(1)}, u32[]{:S(2)}, u32[]{:S(2)}) async-start(bf16[16,2,16384]{2,1,0:T(2,128)(2,1)} %reshape.291), calls=%async_computation.1 | async-start | bytes 2097152 | tf_op jit(solution)/shard_map/all_to_all | solution.py:97
  59.5 78.3 %all-gather = s32[16,6,5]{2,1,0:T(8,128)S(1)} all-gather(s32[1,6,5]{2,1,0:T(8,128)S(1)} %bitcast.75), channel_id=1, replica_groups=mesh['dom'=32,'cls'=16] {'cls'}, dimensions={0}, use_global_device_ids=true | all-gather | bytes 2040 | tf_op jit(solution)/shard_map/all_gather | solution.py:123
  138.5 9.6 %fusion.8 = f32[16,16384]{1,0:T(8,128)} fusion(f32[16,32]{1,0:T(8,128)S(1)} %fusion.48, f32[16384]{0:T(1024)S(1)} %get-tuple-element.20, f32[32]{0:T(128)S(1)} %copy-done.3), kind=kOutput, calls=%fused_computation.12 | convolution fusion | flops 102236160 | bytes 1116288 | tf_op jit(solution)/shard_map/dot_general | solution.py:143
  148.0 0.4 reshape.292
  148.5 4.9 %reshape.296 = bf16[96,16384]{1,0:T(8,128)(2,1)} reshape(bf16[16,6,16384]{2,1,0:T(8,128)(2,1)} %all-gather.4.cloned.1.call-done) | data formatting | bytes 6291456
  153.4 3.5 %fusion.1 = f32[16,16384]{1,0:T(8,128)} fusion(bf16[96,16384]{1,0:T(8,128)(2,1)} %reshape.296, bf16[32,16384]{1,0:T(8,128)(2,1)S(1)} %reshape.292, s32[128]{0:T(128)S(1)} %get-tuple-element.17), kind=kOutput, calls=%fused_computation.4 | convolution fusion | flops 75499520 | bytes 5243392 | tf_op jit(solution)/shard_map/dot_general | solution.py:138
  157.0 141.1 %all-reduce.3.cloned.1.call-done = (f32[16,16384]{1,0:T(8,128)}, f32[16,16384]{1,0:T(8,128)}) async-done(((f32[16,16384]{1,0:T(8,128)}, f32[16,16384]{1,0:T(8,128)}), (f32[16,16384]{1,0:T(8,128)}, f32[16,16384]{1,0:T(8,128)})) %all-reduce.3.cloned.1.call-update) | async-done | bytes 2097168 | tf_op jit(solution)/shard_map/psum | solution.py:144
  298.1 1.7 divide_bitcast_fusion.1
  300.0 1.8 fusion.21
  301.8 1.9 multiply_reduce_fusion
  303.9 1.3 copy.38
  (48 shorter events, 3.4 us)
Async XLA Ops:
  6.5 2.4 copy-start
  6.5 141.9 %all-gather.4.cloned.1.call-start = ((), (), s32[]{:S(2)}) async-start(), calls=%async_computation.2 | async-start | bytes 4456448 | tf_op jit(solution)/shard_map/all_gather | solution.py:122
  13.3 2.3 copy-start.2
  13.4 2.3 copy-start.3
  28.1 27.2 %all-to-all-start = ((s32[16,2,2]{1,2,0:T(2,128)}), s32[16,2,2]{1,2,0:T(2,128)S(1)}, u32[]{:S(2)}, u32[]{:S(2)}) async-start(s32[16,2,2]{1,2,0:T(2,128)} %copy.30), calls=%async_computation | async-start | bytes 32768 | tf_op jit(solution)/shard_map/all_to_all | solution.py:98
  55.3 92.7 %all-to-all-start.1 = ((bf16[16,2,16384]{2,1,0:T(2,128)(2,1)}), bf16[16,2,16384]{2,1,0:T(2,128)(2,1)S(1)}, u32[]{:S(2)}, u32[]{:S(2)}) async-start(bf16[16,2,16384]{2,1,0:T(2,128)(2,1)} %reshape.291), calls=%async_computation.1 | async-start | bytes 2097152 | tf_op jit(solution)/shard_map/all_to_all | solution.py:97
  59.0 239.1 %all-reduce.3.cloned.1.call-start = ((), (), s32[]{:S(2)}) async-start(), calls=%async_computation.3 | async-start | bytes 4194304 | tf_op jit(solution)/shard_map/psum | solution.py:144
  156.9 141.2 %copy-start.1 = (f32[128,128]{1,0:T(8,128)S(1)}, f32[128,128]{1,0:T(8,128)}, u32[]{:S(2)}) copy-start(f32[128,128]{1,0:T(8,128)} %param.11) | copy-start | bytes 196612
Sparse Core Ops, SparseCore 0:
  27.2 119.9 all-gather.3
  157.1 140.9 all-reduce.2
where the time goes:
time: 313 us; the launch traced here: 312 us
  waiting for transfers between devices  150 us (48%)
  blocking collectives  78.3 us (25%)
  matrix products  32.6 us (10%)
  starting transfers between devices  19.4 us (6%)
  between operations  13.6 us (4%)
  local copies, waits for them, and re-layouts  13.3 us (4%)
  other arithmetic  4.4 us (1%)
    psum x1, waiting for transfers between devices, body(): numerator, denominator = lax.psum((numerator, denominator), 'dom')  141 us
    all_gather x1, blocking collectives, body(): lax.all_gather(extra_tags, 'cls', axis=0, tiled=True)  78.3 us
    all_to_all x1, starting transfers between devices, body(): lax.all_to_all(labels, 'cls', split_axis=0, concat_axis=0, tiled=True)  15.7 us
    dot_general x1, matrix products, body(): denominator = jnp.dot(counts, ctf_table, precision=lax.Precision.HIGHEST)  9.57 us
    all_to_all x1, waiting for transfers between devices, body(): lax.all_to_all(labels, 'cls', split_axis=0, concat_axis=0, tiled=True)  9.24 us
    dot_general x1, matrix products, weigh(): jnp.einsum('kux,pxkv->puv', left_table, halves, preferred_element_type=jn...  9.17 us
  transfers between devices with their start and end apart: 4, of which 2 were waited for; matrix products, arithmetic and copies ran while one was open for 5% of the time, Pallas kernels for 0%

commit v1 on v0

v1 whole, which is shorter than its diff:
```python
import functools
import math

import jax
import jax.numpy as jnp
import ml_dtypes
import numpy as np
from jax import lax
from jax.experimental import pallas as pl
from jax.experimental.pallas import tpu as pltpu
from jax.sharding import PartitionSpec as P

SIDE = 128
STACK = 32
OWNED = 16
CLASSES = 256
N_DOM = 32
N_CLS = 16
BINS = 32
REACH = 16
PER = SIDE // N_DOM
ROWS = PER * STACK + 16
WIDE = PER * SIDE
LIMIT = 56 * 1024 * 1024
PHASE = 0.1
EPSILON = 1e-05

VMEM = pl.BlockSpec(memory_space=pltpu.VMEM)
SMEM = pl.BlockSpec(memory_space=pltpu.SMEM)
PARAMS = pltpu.CompilerParams(vmem_limit_bytes=LIMIT)


def hartley_tables():
    indices = np.arange(SIDE)
    angles = ((indices[:, None] * indices[None, :]) % SIDE).astype(np.float32)
    angles = angles * np.float32(2.0 * math.pi / SIDE)
    return np.cos(angles).astype(np.float32), np.sin(angles).astype(np.float32)


def forward_tables():
    cosine, sine = hartley_tables()
    factor = np.float32(1.0 / math.sqrt(SIDE))
    right = (np.concatenate([cosine + sine, cosine - sine], axis=1) * factor).astype(ml_dtypes.bfloat16)
    left_cos = (cosine * factor).astype(ml_dtypes.bfloat16)
    left_sin = (sine * factor).astype(ml_dtypes.bfloat16)
    indices = np.arange(SIDE)
    rights, lefts = [], []
    for shift in range(-REACH, REACH + 1):
        moved = (indices + shift) % SIDE
        rights.append(right[moved])
        lefts.append(np.concatenate([left_cos[:, moved], left_sin[:, moved]], axis=1))
    return np.stack(rights), np.stack(lefts)


def split(table):
    high = table.astype(ml_dtypes.bfloat16)
    low = (table - high.astype(np.float32)).astype(ml_dtypes.bfloat16)
    return high, low


def inverse_tables():
    cosine, sine = hartley_tables()
    left_high, left_low = split(np.concatenate([cosine, sine], axis=0))
    left = np.concatenate([left_high, left_low], axis=1)
    right_high, right_low = split(np.concatenate([cosine + sine, cosine - sine], axis=0))
    return left, right_high, right_low


def forward_kernel(shifts, bins, images, rights, lefts, ctf, tags, out, spectra):
    def particle(p, carry):
        right = rights[shifts[p, 1] + REACH]
        left = lefts[shifts[p, 0] + REACH]
        halves = jnp.dot(images[p], right, preferred_element_type=jnp.float32).astype(jnp.bfloat16)
        stacked = jnp.concatenate([halves[:, :SIDE], halves[:, SIDE:]], axis=0)
        spectrum = jnp.dot(left, stacked, preferred_element_type=jnp.float32)
        start = pl.multiple_of(p * SIDE, SIDE)
        spectra[pl.ds(start, SIDE), :] = ctf[bins[p]] * spectrum
        return carry

    lax.fori_loop(0, STACK, particle, 0, unroll=4)
    for u in range(SIDE):
        j, d = u // N_DOM, u % N_DOM
        row = spectra[pl.ds(u, STACK, stride=SIDE), :]
        out[d, j * STACK : (j + 1) * STACK, :] = row.astype(jnp.bfloat16)
    tile = tags[...]
    for d in range(N_DOM):
        out[d, PER * STACK :, :] = tile


def gather_kernel(arrived, out):
    together = N_DOM // 8
    sums = jnp.zeros((CLASSES, WIDE), jnp.float32)
    counts = jnp.zeros((CLASSES, SIDE), jnp.float32)
    classes = lax.broadcasted_iota(jnp.int32, (CLASSES, SIDE), 0).astype(jnp.float32)
    levels = lax.broadcasted_iota(jnp.int32, (SIDE, SIDE), 0)
    levels = jnp.where(levels < 2 * BINS, levels % BINS, -1).astype(jnp.float32)
    for pair in range(4):
        picks, blocks = [], []
        for g in (2 * pair, 2 * pair + 1):
            tag = sum(
                arrived[g * together + k, PER * STACK :, :].astype(jnp.float32)
                for k in range(together)
            )
            pick = jnp.where(classes == tag[0:1, :], 1.0, 0.0).astype(jnp.bfloat16)
            level = jnp.where(levels == tag[1:2, :], 1.0, 0.0).astype(jnp.bfloat16)
            counts += lax.dot_general(
                pick, level, (((1,), (1,)), ((), ())), preferred_element_type=jnp.float32
            )
            picks.append(pick)
            blocks.append(
                jnp.concatenate(
                    [
                        jnp.concatenate(
                            [
                                arrived[g * together + k, j * STACK : (j + 1) * STACK, :]
                                for k in range(together)
                            ],
                            axis=0,
                        )
                        for j in range(PER)
                    ],
                    axis=1,
                )
            )
        sums += jnp.dot(
            jnp.concatenate(picks, axis=1),
            jnp.concatenate(blocks, axis=0),
            preferred_element_type=jnp.float32,
        )
    lanes = lax.broadcasted_iota(jnp.int32, (CLASSES, SIDE), 1)
    high = jnp.floor(counts * (1.0 / 32.0))
    digits = jnp.where(lanes < BINS, counts - 32.0 * high, high)
    out[:, :WIDE] = sums.astype(jnp.bfloat16)
    out[:, WIDE:] = digits.astype(jnp.bfloat16)


def average_kernel(arrived, squares, regular, out):
    total = arrived[0].astype(jnp.float32)
    for z in range(1, N_CLS):
        total += arrived[z].astype(jnp.float32)
    denominator = jnp.dot(
        total[:, WIDE:],
        squares[...],
        precision=lax.Precision.HIGHEST,
        preferred_element_type=jnp.float32,
    )
    average = total[:, :WIDE] / (denominator + regular[...])
    average = jnp.concatenate(
        [average[:, j * SIDE : (j + 1) * SIDE] for j in range(PER)], axis=0
    ).astype(jnp.bfloat16)
    for d in range(N_DOM):
        out[d] = average


def invert_kernel(arrived, left, right, out, rows):
    count = PER * OWNED
    for d in range(N_DOM):
        rows[d * count : (d + 1) * count, :] = arrived[d].astype(jnp.float32)

    def picture(k):
        parts = [rows[pl.ds(j * OWNED + k, N_DOM, stride=count), :] for j in range(PER)]
        return jnp.concatenate(parts, axis=0).astype(jnp.bfloat16)

    for k in range(0, OWNED, 2):
        both = jnp.concatenate([picture(k), picture(k + 1)], axis=1)
        first = jnp.dot(
            left[...], jnp.concatenate([both, both], axis=0), preferred_element_type=jnp.float32
        ).astype(jnp.bfloat16)
        for i in range(2):
            half = first[:, i * SIDE : (i + 1) * SIDE]
            wide = jnp.concatenate([half[:SIDE], half[SIDE:]], axis=1)
            real = jnp.dot(wide, right[...], preferred_element_type=jnp.float32)
            power = jnp.sum(real * real, axis=0, keepdims=True)
            power = jnp.sum(power, axis=1, keepdims=True) * (1.0 / (SIDE * SIDE))
            out[k + i] = real * (1.0 / jnp.sqrt(power + EPSILON))


def body(images, class_ids, shifts, defocus_bins, defocus, regular):
    dom = lax.axis_index("dom")
    indices = np.arange(SIDE)
    signed = np.where(indices < SIDE // 2, indices, indices - SIDE).astype(np.float32) / SIDE
    squared = jnp.asarray((signed * signed).astype(np.float32))
    along = defocus[:, None] * squared[None, :]
    sin_u, cos_u = jnp.sin(along + PHASE), jnp.cos(along + PHASE)
    sin_v, cos_v = jnp.sin(along), jnp.cos(along)
    ctf = -(sin_u[:, :, None] * cos_v[:, None, :] + cos_u[:, :, None] * sin_v[:, None, :])

    def own(table):
        return lax.dynamic_slice_in_dim(
            table.reshape(*table.shape[:-1], PER, N_DOM), dom, 1, axis=-1
        )

    mine = own(sin_u) * cos_v[:, None, :] + own(cos_u) * sin_v[:, None, :]
    mine = (mine * mine).reshape(BINS, WIDE)
    squares = jnp.concatenate(
        [mine, 32.0 * mine, jnp.zeros((SIDE - 2 * BINS, WIDE), jnp.float32)], axis=0
    )
    own_regular = lax.dynamic_slice_in_dim(
        regular.reshape(PER, N_DOM, SIDE), dom, 1, axis=1
    ).reshape(1, WIDE)

    lanes = jnp.arange(SIDE, dtype=jnp.int32)
    here = (lanes // STACK == dom % 4)[None, :]
    numbers = jnp.stack([class_ids, defocus_bins]).astype(jnp.bfloat16)
    tags = jnp.where(here, jnp.tile(numbers, (1, 4)), jnp.bfloat16(0))
    tags = jnp.concatenate([tags, jnp.zeros((14, SIDE), jnp.bfloat16)], axis=0)

    rights, lefts = forward_tables()
    payload = pl.pallas_call(
        forward_kernel,
        out_shape=jax.ShapeDtypeStruct((N_DOM, ROWS, SIDE), jnp.bfloat16),
        in_specs=[SMEM, SMEM, VMEM, VMEM, VMEM, VMEM, VMEM],
        out_specs=VMEM,
        scratch_shapes=[pltpu.VMEM((STACK * SIDE, SIDE), jnp.float32)],
        compiler_params=PARAMS,
    )(shifts, defocus_bins, images, jnp.asarray(rights), jnp.asarray(lefts), ctf, tags)

    arrived = lax.all_to_all(payload, "dom", split_axis=0, concat_axis=0, tiled=True)
    sums = pl.pallas_call(
        gather_kernel,
        out_shape=jax.ShapeDtypeStruct((CLASSES, WIDE + SIDE), jnp.bfloat16),
        in_specs=[VMEM],
        out_specs=VMEM,
        compiler_params=PARAMS,
    )(arrived)

    arrived = lax.all_to_all(
        sums.reshape(N_CLS, OWNED, WIDE + SIDE), "cls", split_axis=0, concat_axis=0, tiled=True
    )
    averages = pl.pallas_call(
        average_kernel,
        out_shape=jax.ShapeDtypeStruct((N_DOM, PER * OWNED, SIDE), jnp.bfloat16),
        in_specs=[VMEM, VMEM, VMEM],
        out_specs=VMEM,
        compiler_params=PARAMS,
    )(arrived, squares, own_regular)

    arrived = lax.all_to_all(averages, "dom", split_axis=0, concat_axis=0, tiled=True)
    left, right, _ = inverse_tables()
    return pl.pallas_call(
        invert_kernel,
        out_shape=jax.ShapeDtypeStruct((OWNED, SIDE, SIDE), jnp.float32),
        in_specs=[VMEM, VMEM, VMEM],
        out_specs=VMEM,
        scratch_shapes=[pltpu.VMEM((N_DOM * PER * OWNED, SIDE), jnp.float32)],
        compiler_params=PARAMS,
    )(arrived, jnp.asarray(left), jnp.asarray(right))


def solution(mesh):
    in_specs = (
        P(("dom", "cls"), None, None),
        P(("dom", "cls")),
        P(("dom", "cls"), None),
        P(("dom", "cls")),
        P(),
        P(),
    )
    return jax.shard_map(
        body, mesh=mesh, in_specs=in_specs, out_specs=P("cls", None, None), check_vma=False
    )
```

time: 313 us -> 105 us (0.34)
  waiting for transfers between devices: 150 us -> 13.3 us
  matrix products: 32.6 us -> 0 us
  blocking collectives: 78.3 us -> 53 us
  Pallas kernels: 0 us -> 17.1 us
  between operations: 13.6 us -> 0.08 us
  local copies, waits for them, and re-layouts: 13.3 us -> 3.68 us
  starting transfers between devices: 19.4 us -> 12.3 us
    psum x1 -> x0, waiting for transfers between devices: 141 us -> none  [body(): numerator, denominator = lax.psum((numerator, denominator), 'dom')]
    all_gather x1 -> x0, blocking collectives: 78.3 us -> none  [body(): lax.all_gather(extra_tags, 'cls', axis=0, tiled=True)]
    all_to_all x0 -> x2, blocking collectives: none -> 53 us  [the longest x1 30.3 us: body(): lax.all_to_all(payload, 'dom', split_axis=0, concat_axis=0, tiled=True)]
    dot_general x10 -> x0, matrix products: 32.6 us -> none  [the longest x1 9.57 us: body(): denominator = jnp.dot(counts, ctf_table, precision=lax.Precision.HIGHEST)]
    pallas_call x0 -> x4, Pallas kernels: none -> 17.1 us  [the longest x1 8.77 us: body(): pl.pallas_call(forward_kernel, out_shape=jax.ShapeDtypeStruct((N_DOM, ROW...]
    all_to_all x2 -> x1, starting transfers between devices: 19.4 us -> 12.3 us  [body(): lax.all_to_all(sums.reshape(N_CLS, OWNED, WIDE + SIDE), 'cls', split_axis...]
    all_to_all x2 -> x1, waiting for transfers between devices: 9.24 us -> 13.3 us  [body(): lax.all_to_all(sums.reshape(N_CLS, OWNED, WIDE + SIDE), 'cls', split_axis...]
    reshape x4 -> x1, local copies, waits for them, and re-layouts: 4.09 us -> 0.59 us  [body(): own_regular = lax.dynamic_slice_in_dim(regular.reshape(PER, N_DOM, SIDE),...]
  transfers between devices with their start and end apart: 4 -> 1, of which waited for: 2 -> 1; matrix products, arithmetic and copies ran while one was open for 5% -> 2% of each run, Pallas kernels for 0% -> 0%
where the time goes in v1:
time: 105 us; the launch traced here: 104 us
  blocking collectives  53 us (50%)
  Pallas kernels  17.1 us (16%)
  waiting for transfers between devices  13.3 us (13%)
  starting transfers between devices  12.3 us (12%)
  other arithmetic  4.92 us (5%)
  local copies, waits for them, and re-layouts  3.68 us (4%)
    all_to_all x1, blocking collectives, body(): lax.all_to_all(payload, 'dom', split_axis=0, concat_axis=0, tiled=True)  30.3 us
    all_to_all x1, blocking collectives, body(): lax.all_to_all(averages, 'dom', split_axis=0, concat_axis=0, tiled=True)  22.7 us
    all_to_all x1, waiting for transfers between devices, body(): lax.all_to_all(sums.reshape(N_CLS, OWNED, WIDE + SIDE), 'cls', split_axis...  13.3 us
    all_to_all x1, starting transfers between devices, body(): lax.all_to_all(sums.reshape(N_CLS, OWNED, WIDE + SIDE), 'cls', split_axis...  12.3 us
    pallas_call x1, Pallas kernels, body(): pl.pallas_call(forward_kernel, out_shape=jax.ShapeDtypeStruct((N_DOM, ROW...  8.77 us
    pallas_call x1, Pallas kernels, body(): pl.pallas_call(invert_kernel, out_shape=jax.ShapeDtypeStruct((OWNED, SIDE...  3.57 us
    pallas_call x1, Pallas kernels, body(): pl.pallas_call(gather_kernel, out_shape=jax.ShapeDtypeStruct((CLASSES, WI...  2.58 us
    neg x1, other arithmetic, body(): -(sin_u[:, :, None] * cos_v[:, None, :] + cos_u[:, :, None] * sin_v[:, No...  2.28 us
  transfers between devices with their start and end apart: 1, of which 1 were waited for; matrix products, arithmetic and copies ran while one was open for 2% of the time, Pallas kernels for 0%

profile of v1, /device:TPU:1, one launch (start us, length us, event | category | flops | bytes accessed | tf_op | source)
XLA Modules:
  0.0 104.4 jit_solution(3345680250611675421)
XLA Ops:
  0.0 0.0 copy-start
  0.0 0.7 convert_bitcast_fusion
  0.7 0.1 tile.10
  0.8 1.4 %copy.12.shifts = s32[32,2]{1,0:T(8,128)} copy(s32[32,2]{0,1:T(2,128)} %param.13) | data formatting | bytes 512 | tf_op args[2]
  2.2 0.6 concatenate.11.tags
  2.8 0.9 fusion.1
  3.7 2.3 %add_negate_fusion.ctf = f32[32,128,128]{2,1,0:T(8,128)} fusion(f32[32,128]{1,0:T(8,128)S(1)} %get-tuple-element.8, f32[32,128]{1,0:T(8,128)S(1)} %get-tuple-element.10, f32[32,128]{1,0:T(8,128)S(1)} %get-tuple-element.9, f32[32,128]{1,0:T(8,128)S(1)} %get-tuple-element.7), kind=kLoop, calls=%fused_computation | loop fusion | flops 2097152 | bytes 2162688 | tf_op jit(solution)/shard_map/neg | solution.py:186
  5.9 8.8 %shard_map.109 = bf16[32,144,128]{2,1,0:T(8,128)(2,1)} custom-call(s32[32,2]{1,0:T(8,128)} %copy.12.shifts, s32[32]{0:T(128)} %bins.1, bf16[32,128,128]{2,1,0:T(8,128)(2,1)} %images.1, bf16[33,128,256]{2,1,0:T(8,128)(2,1)} %constant.58.clone.rights, bf16[33,128,256]{2,1,0:T(8,128)(2,1)} %constant.59.clone.lefts, f32[32,128,128]{2,1,0:T(8,128)} %add_negate_fusion.ctf, ...), custom_call_target="tpu_custom_call" | custom-call | tf_op jit(solution)/shard_map/pallas_call | solution.py:209
  14.7 30.3 %all_to_all.15.arrived = bf16[32,144,128]{2,1,0:T(8,128)(2,1)} all-to-all(bf16[32,144,128]{2,1,0:T(8,128)(2,1)} %shard_map.109), channel_id=1, replica_groups=mesh['dom'=32,'cls'=16] {'dom'}, dimensions={0} | all-to-all | bytes 2359296 | tf_op jit(solution)/shard_map/all_to_all | solution.py:218
  45.1 2.6 %shard_map.110 = bf16[256,640]{1,0:T(8,128)(2,1)} custom-call(bf16[32,144,128]{2,1,0:T(8,128)(2,1)} %all_to_all.15.arrived), custom_call_target="tpu_custom_call" | custom-call | tf_op jit(solution)/shard_map/pallas_call | solution.py:219
  47.7 12.3 %all-to-all-start.1 = ((bf16[16,16,640]{2,1,0:T(8,128)(2,1)}), bf16[16,16,640]{2,1,0:T(8,128)(2,1)S(1)}, u32[]{:S(2)}, u32[]{:S(2)}) async-start(bf16[16,16,640]{2,1,0:T(8,128)(2,1)} %bitcast.21), calls=%async_computation.1 | async-start | bytes 655360 | tf_op jit(solution)/shard_map/all_to_all | solution.py:227
  60.0 0.1 multiply_add_fusion
  60.2 0.1 copy.13
  60.2 0.1 copy.14
  60.3 0.1 add_multiply_fusion
  60.5 0.1 pad.3.clone
  60.6 0.0 copy-done
  60.6 0.6 dynamic-slice_bitcast_fusion.regular
  61.2 0.8 maximum_maximum_fusion.squares
  62.0 13.3 %all-to-all-done.1.arrived = bf16[16,16,640]{2,1,0:T(8,128)(2,1)S(1)} async-done(((bf16[16,16,640]{2,1,0:T(8,128)(2,1)}), bf16[16,16,640]{2,1,0:T(8,128)(2,1)S(1)}, u32[]{:S(2)}, u32[]{:S(2)}) %all-to-all-start.1) | async-done | bytes 327712 | tf_op jit(solution)/shard_map/all_to_all | solution.py:227
  75.3 0.7 copy-done.1
  76.0 2.2 %shard_map.111 = bf16[32,64,128]{2,1,0:T(8,128)(2,1)} custom-call(bf16[16,16,640]{2,1,0:T(8,128)(2,1)} %copy-done.1, f32[128,512]{1,0:T(8,128)} %maximum_maximum_fusion.squares, f32[1,512]{1,0:T(1,128)} %dynamic-slice_bitcast_fusion.regular), custom_call_target="tpu_custom_call" | custom-call | tf_op jit(solution)/shard_map/pallas_call | solution.py:230
  78.2 22.7 %all_to_all.16.arrived = bf16[32,64,128]{2,1,0:T(8,128)(2,1)} all-to-all(bf16[32,64,128]{2,1,0:T(8,128)(2,1)} %shard_map.111), channel_id=1, replica_groups=mesh['dom'=32,'cls'=16] {'dom'}, dimensions={0} | all-to-all | bytes 1048576 | tf_op jit(solution)/shard_map/all_to_all | solution.py:238
  100.9 3.6 %shard_map.112 = f32[16,128,128]{2,1,0:T(8,128)} custom-call(bf16[32,64,128]{2,1,0:T(8,128)(2,1)} %all_to_all.16.arrived, bf16[256,256]{1,0:T(8,128)(2,1)} %constant.60.clone.left, bf16[256,128]{1,0:T(8,128)(2,1)} %constant.61.clone.right), custom_call_target="tpu_custom_call" | custom-call | tf_op jit(solution)/shard_map/pallas_call | solution.py:240
  (13 shorter events, 0.1 us)
Async XLA Ops:
  0.0 60.6 %copy-start = (f32[128,128]{1,0:T(8,128)S(1)}, f32[128,128]{1,0:T(8,128)}, u32[]{:S(2)}) copy-start(f32[128,128]{1,0:T(8,128)} %param.16) | copy-start | bytes 196612
  14.7 45.3 %copy-start.2 = (f32[4,32]{0,1:T(8,128)S(1)}, f32[4,32]{0,1:T(8,128)}, u32[]{:S(2)}) copy-start(f32[4,32]{0,1:T(8,128)} %constant.68) | copy-start | bytes 1540
  14.7 45.3 %copy-start.3 = (f32[32]{0:T(128)S(1)}, f32[32]{0:T(128)}, u32[]{:S(2)}) copy-start(f32[32]{0:T(128)} %param.15) | copy-start | bytes 388
  47.7 27.6 %all-to-all-start.1 = ((bf16[16,16,640]{2,1,0:T(8,128)(2,1)}), bf16[16,16,640]{2,1,0:T(8,128)(2,1)S(1)}, u32[]{:S(2)}, u32[]{:S(2)}) async-start(bf16[16,16,640]{2,1,0:T(8,128)(2,1)} %bitcast.21), calls=%async_computation.1 | async-start | bytes 655360 | tf_op jit(solution)/shard_map/all_to_all | solution.py:227
  75.3 0.7 copy-start.1

commit v2 on v1

v2 whole, which is shorter than its diff:
```python
import math

import jax
import jax.numpy as jnp
import ml_dtypes
import numpy as np
from jax import lax
from jax.experimental import pallas as pl
from jax.experimental.pallas import tpu as pltpu
from jax.sharding import PartitionSpec as P

SIDE = 128
STACK = 32
OWNED = 16
CLASSES = 256
N_DOM = 32
N_CLS = 16
BINS = 32
REACH = 16
PER = SIDE // N_DOM
ROWS = PER * STACK + 16
WIDE = PER * SIDE
GROUP = 16
APART = SIDE + 8
SPREAD = PER * OWNED + 8
PHASE = 0.1
EPSILON = 1e-05

VMEM = pl.BlockSpec(memory_space=pltpu.VMEM)
HBM = pl.BlockSpec(memory_space=pl.ANY)
SMEM = pl.BlockSpec(memory_space=pltpu.SMEM)
ALL = pltpu.CompilerParams(vmem_limit_bytes=60 * 1024 * 1024)
PARAMS = pltpu.CompilerParams(vmem_limit_bytes=16 * 1024 * 1024)


def hartley_tables():
    indices = np.arange(SIDE)
    angles = ((indices[:, None] * indices[None, :]) % SIDE).astype(np.float32)
    angles = angles * np.float32(2.0 * math.pi / SIDE)
    return np.cos(angles).astype(np.float32), np.sin(angles).astype(np.float32)


def forward_tables():
    cosine, sine = hartley_tables()
    factor = np.float32(1.0 / math.sqrt(SIDE))
    right = (np.concatenate([cosine + sine, cosine - sine], axis=1) * factor).astype(ml_dtypes.bfloat16)
    left = (np.concatenate([cosine, sine], axis=1) * factor).astype(ml_dtypes.bfloat16)
    return right, left


def split(table):
    high = table.astype(ml_dtypes.bfloat16)
    low = (table - high.astype(np.float32)).astype(ml_dtypes.bfloat16)
    return high, low


def inverse_tables():
    cosine, sine = hartley_tables()
    left_high, left_low = split(np.concatenate([cosine, sine], axis=0))
    left = np.concatenate([left_high, left_low], axis=1)
    right_high, right_low = split(np.concatenate([cosine + sine, cosine - sine], axis=0))
    return left, right_high, right_low


def forward_kernel(
    shifts, bins, class_ids, defocus, images, right, left, out, pictures, moved, spectra, trig, sems
):
    def picture_copy(g):
        part = pl.ds(g * GROUP, GROUP)
        return pltpu.make_async_copy(images.at[part], pictures.at[part], sems.at[g])

    for g in range(STACK // GROUP):
        picture_copy(g).start()

    lane = lax.broadcasted_iota(jnp.int32, (SIDE, SIDE), 1)
    line = lax.broadcasted_iota(jnp.int32, (SIDE, SIDE), 0)

    def squared(index):
        signed = jnp.where(index < SIDE // 2, index, index - SIDE).astype(jnp.float32) * (1.0 / SIDE)
        return signed * signed

    by_lane = jnp.zeros((1, SIDE), jnp.float32)
    by_line = jnp.zeros((BINS, SIDE), jnp.float32)
    for b in range(BINS):
        level = defocus[b]
        by_lane = jnp.where(lane[:1] == b, level, by_lane)
        by_line = jnp.where(line[:BINS] == b, level, by_line)
    angles = jnp.concatenate(
        [squared(line) * by_lane + PHASE, squared(lane[:BINS]) * by_line], axis=0
    )
    trig[0] = jnp.sin(angles)
    trig[1] = jnp.cos(angles)

    tag_class = jnp.zeros((1, SIDE), jnp.int32)
    tag_bin = jnp.zeros((1, SIDE), jnp.int32)
    first = lax.rem(lax.axis_index("dom"), 4) * STACK
    for p in range(STACK):
        tag_class = jnp.where(lane[:1] == first + p, class_ids[p], tag_class)
        tag_bin = jnp.where(lane[:1] == first + p, bins[p], tag_bin)
    tile = jnp.where(line[:16] == 0, tag_class, jnp.where(line[:16] == 1, tag_bin, 0))
    tile = tile.astype(jnp.float32).astype(jnp.bfloat16)
    for d in range(N_DOM):
        out[d, PER * STACK :, :] = tile

    def group(g, carry):
        picture_copy(g).wait()
        shifted = []
        for i in range(GROUP):
            p = g * GROUP + i
            picture = pictures[p].astype(jnp.float32)
            picture = pltpu.roll(picture, lax.rem(shifts[1, p] + SIDE, SIDE), axis=1)
            moved[i, REACH : REACH + SIDE, :] = picture
            moved[i, :REACH, :] = picture[SIDE - REACH :]
            moved[i, REACH + SIDE :, :] = picture[:REACH]
            shifted.append(moved[i, pl.ds(REACH - shifts[0, p], SIDE), :].astype(jnp.bfloat16))
        halves = jnp.dot(
            jnp.concatenate(shifted, axis=0), right[...], preferred_element_type=jnp.float32
        ).astype(jnp.bfloat16)
        for i in range(0, GROUP, 2):
            one = halves[i * SIDE : (i + 1) * SIDE]
            two = halves[(i + 1) * SIDE : (i + 2) * SIDE]
            both = jnp.concatenate(
                [
                    jnp.concatenate([one[:, :SIDE], two[:, :SIDE]], axis=1),
                    jnp.concatenate([one[:, SIDE:], two[:, SIDE:]], axis=1),
                ],
                axis=0,
            )
            spectrum = jnp.dot(left[...], both, preferred_element_type=jnp.float32)
            for k in range(2):
                p = g * GROUP + i + k
                level = bins[p]
                which = jnp.full((SIDE, SIDE), level, jnp.int32)
                sin_u = jnp.take_along_axis(trig[0, :SIDE], which, axis=1)
                cos_u = jnp.take_along_axis(trig[1, :SIDE], which, axis=1)
                sin_v = trig[0, pl.ds(SIDE + level, 1), :]
                cos_v = trig[1, pl.ds(SIDE + level, 1), :]
                ctf = -(sin_u * cos_v + cos_u * sin_v)
                start = pl.multiple_of(p * APART, 8)
                spectra[pl.ds(start, SIDE), :] = ctf * spectrum[:, k * SIDE : (k + 1) * SIDE]
        return carry

    lax.fori_loop(0, STACK // GROUP, group, 0)
    for u in range(SIDE):
        j, d = u // N_DOM, u % N_DOM
        row = spectra[pl.ds(u, STACK, stride=APART), :]
        out[d, j * STACK : (j + 1) * STACK, :] = row.astype(jnp.bfloat16)


def gather_kernel(arrived, out):
    together = SIDE // STACK
    classes = lax.broadcasted_iota(jnp.int32, (CLASSES, SIDE), 0).astype(jnp.float32)
    levels = (lax.broadcasted_iota(jnp.int32, (SIDE, SIDE), 0) % BINS).astype(jnp.float32)
    picks, lots, blocks = [], [], []
    for g in range(N_DOM // together):
        members = range(g * together, (g + 1) * together)
        tag = sum(arrived[s, PER * STACK :, :].astype(jnp.float32) for s in members)
        picks.append(jnp.where(classes == tag[0:1, :], 1.0, 0.0).astype(jnp.bfloat16))
        lots.append(jnp.where(levels == tag[1:2, :], 1.0, 0.0).astype(jnp.bfloat16))
        parts = [
            jnp.concatenate([arrived[s, j * STACK : (j + 1) * STACK, :] for s in members], axis=0)
            for j in range(PER)
        ]
        blocks.append(jnp.concatenate(parts, axis=1))
    pick = jnp.concatenate(picks, axis=1)
    sums = jnp.dot(pick, jnp.concatenate(blocks, axis=0), preferred_element_type=jnp.float32)
    counts = lax.dot_general(
        pick,
        jnp.concatenate(lots, axis=1),
        (((1,), (1,)), ((), ())),
        preferred_element_type=jnp.float32,
    )
    lanes = lax.broadcasted_iota(jnp.int32, (CLASSES, SIDE), 1)
    high = jnp.floor(counts * (1.0 / 32.0))
    digits = jnp.where(lanes % (2 * BINS) < BINS, counts - 32.0 * high, high)
    out[:, :WIDE] = sums.astype(jnp.bfloat16)
    out[:, WIDE:] = digits.astype(jnp.bfloat16)


def average_kernel(arrived, squares, regular, out):
    total = arrived[0].astype(jnp.float32)
    for z in range(1, N_CLS):
        total += arrived[z].astype(jnp.float32)
    lanes = lax.broadcasted_iota(jnp.int32, (OWNED, SIDE), 1)
    even = lanes % (2 * BINS) < BINS
    digits = total[:, WIDE:]
    ahead = pltpu.roll(digits, SIDE - BINS, axis=1)
    behind = pltpu.roll(digits, BINS, axis=1)
    counts = jnp.where(even, digits + 32.0 * ahead, behind + 32.0 * digits)
    high = jnp.floor(counts * (1.0 / 128.0))
    digits = jnp.where(even, counts - 128.0 * high, high).astype(jnp.bfloat16)
    denominator = jnp.dot(digits, squares[...], preferred_element_type=jnp.float32)
    average = total[:, :WIDE] / (denominator + regular[...])
    average = jnp.concatenate(
        [average[:, j * SIDE : (j + 1) * SIDE] for j in range(PER)], axis=0
    ).astype(jnp.bfloat16)
    for d in range(N_DOM):
        out[d] = average


def invert_kernel(arrived, left, right, out, rows):
    count = PER * OWNED
    for d in range(N_DOM):
        rows[d * SPREAD : d * SPREAD + count, :] = arrived[d].astype(jnp.float32)

    def picture(k):
        parts = [rows[pl.ds(j * OWNED + k, N_DOM, stride=SPREAD), :] for j in range(PER)]
        return jnp.concatenate(parts, axis=0).astype(jnp.bfloat16)

    for k in range(0, OWNED, 2):
        both = jnp.concatenate([picture(k), picture(k + 1)], axis=1)
        first = jnp.dot(
            left[...], jnp.concatenate([both, both], axis=0), preferred_element_type=jnp.float32
        ).astype(jnp.bfloat16)
        wide = jnp.concatenate(
            [
                jnp.concatenate([first[:SIDE, :SIDE], first[SIDE:, :SIDE]], axis=1),
                jnp.concatenate([first[:SIDE, SIDE:], first[SIDE:, SIDE:]], axis=1),
            ],
            axis=0,
        )
        pair = jnp.dot(wide, right[...], preferred_element_type=jnp.float32)
        for i in range(2):
            real = pair[i * SIDE : (i + 1) * SIDE]
            power = jnp.sum(real * real, axis=0, keepdims=True)
            power = jnp.sum(power, axis=1, keepdims=True) * (1.0 / (SIDE * SIDE))
            out[k + i] = real * (1.0 / jnp.sqrt(power + EPSILON))


def body(images, class_ids, shifts, defocus_bins, defocus, regular):
    dom = lax.axis_index("dom")
    indices = np.arange(SIDE)
    signed = np.where(indices < SIDE // 2, indices, indices - SIDE).astype(np.float32) / SIDE
    squared = jnp.asarray((signed * signed).astype(np.float32))
    along = defocus[:, None] * squared[None, :]
    sin_u, cos_u = jnp.sin(along + PHASE), jnp.cos(along + PHASE)
    sin_v, cos_v = jnp.sin(along), jnp.cos(along)

    def own(table):
        return lax.dynamic_slice_in_dim(
            table.reshape(*table.shape[:-1], PER, N_DOM), dom, 1, axis=-1
        )

    mine = own(sin_u) * cos_v[:, None, :] + own(cos_u) * sin_v[:, None, :]
    mine = (mine * mine).reshape(BINS, WIDE)
    high = mine.astype(jnp.bfloat16)
    low = (mine - high.astype(jnp.float32)).astype(jnp.bfloat16)
    squares = jnp.concatenate([high, 128 * high, low, 128 * low], axis=0)
    own_regular = lax.dynamic_slice_in_dim(
        regular.reshape(PER, N_DOM, SIDE), dom, 1, axis=1
    ).reshape(1, WIDE)

    right, left = forward_tables()
    payload = pl.pallas_call(
        forward_kernel,
        out_shape=jax.ShapeDtypeStruct((N_DOM, ROWS, SIDE), jnp.bfloat16),
        in_specs=[SMEM, SMEM, SMEM, SMEM, HBM, VMEM, VMEM],
        out_specs=VMEM,
        scratch_shapes=[
            pltpu.VMEM((STACK, SIDE, SIDE), jnp.bfloat16),
            pltpu.VMEM((GROUP, SIDE + 2 * REACH, SIDE), jnp.float32),
            pltpu.VMEM((STACK * APART, SIDE), jnp.float32),
            pltpu.VMEM((2, SIDE + BINS, SIDE), jnp.float32),
            pltpu.SemaphoreType.DMA((STACK // GROUP,)),
        ],
        compiler_params=ALL,
    )(shifts.T, defocus_bins, class_ids, defocus, images, jnp.asarray(right), jnp.asarray(left))

    arrived = lax.all_to_all(payload, "dom", split_axis=0, concat_axis=0, tiled=True)
    sums = pl.pallas_call(
        gather_kernel,
        out_shape=jax.ShapeDtypeStruct((CLASSES, WIDE + SIDE), jnp.bfloat16),
        in_specs=[VMEM],
        out_specs=VMEM,
        compiler_params=PARAMS,
    )(arrived)

    arrived = lax.all_to_all(
        sums.reshape(N_CLS, OWNED, WIDE + SIDE), "cls", split_axis=0, concat_axis=0, tiled=True
    )
    averages = pl.pallas_call(
        average_kernel,
        out_shape=jax.ShapeDtypeStruct((N_DOM, PER * OWNED, SIDE), jnp.bfloat16),
        in_specs=[VMEM, VMEM, VMEM],
        out_specs=VMEM,
        compiler_params=PARAMS,
    )(arrived, squares, own_regular)

    arrived = lax.all_to_all(averages, "dom", split_axis=0, concat_axis=0, tiled=True)
    left, right, _ = inverse_tables()
    return pl.pallas_call(
        invert_kernel,
        out_shape=jax.ShapeDtypeStruct((OWNED, SIDE, SIDE), jnp.float32),
        in_specs=[VMEM, VMEM, VMEM],
        out_specs=VMEM,
        scratch_shapes=[pltpu.VMEM((N_DOM * SPREAD, SIDE), jnp.float32)],
        compiler_params=PARAMS,
    )(arrived, jnp.asarray(left), jnp.asarray(right))


def solution(mesh):
    in_specs = (
        P(("dom", "cls"), None, None),
        P(("dom", "cls")),
        P(("dom", "cls"), None),
        P(("dom", "cls")),
        P(),
        P(),
    )
    return jax.shard_map(
        body, mesh=mesh, in_specs=in_specs, out_specs=P("cls", None, None), check_vma=False
    )
```

time: 105 us -> 88.1 us (0.84)
  blocking collectives: 53 us -> 21.4 us
  waiting for transfers between devices: 13.3 us -> 33.2 us
  starting transfers between devices: 12.3 us -> 23.4 us
  Pallas kernels: 17.1 us -> 8.95 us
  other arithmetic: 4.92 us -> 0.4 us
  local copies, waits for them, and re-layouts: 3.68 us -> 0.29 us
    all_to_all x1 -> x0, blocking collectives: 30.3 us -> none  [body(): lax.all_to_all(payload, 'dom', split_axis=0, concat_axis=0, tiled=True)]
    all_to_all x0 -> x1, waiting for transfers between devices: none -> 18.4 us  [body(): lax.all_to_all(payload, 'dom', split_axis=0, concat_axis=0, tiled=True)]
    all_to_all x0 -> x1, starting transfers between devices: none -> 10.5 us  [body(): lax.all_to_all(payload, 'dom', split_axis=0, concat_axis=0, tiled=True)]
    pallas_call x1, Pallas kernels: 8.77 us -> 5.23 us  [body(): pl.pallas_call(forward_kernel, out_shape=jax.ShapeDtypeStruct((N_DOM, ROW...]
    neg x1 -> x0, other arithmetic: 2.28 us -> none  [body(): -(sin_u[:, :, None] * cos_v[:, None, :] + cos_u[:, :, None] * sin_v[:, No...]
    unnamed x10 -> x13, local copies, waits for them, and re-layouts: 2.1 us -> 0.05 us
    pallas_call x1, Pallas kernels: 2.18 us -> 0.27 us  [body(): pl.pallas_call(average_kernel, out_shape=jax.ShapeDtypeStruct((N_DOM, PER...]
    all_to_all x1, waiting for transfers between devices: 13.3 us -> 14.8 us  [body(): lax.all_to_all(sums.reshape(N_CLS, OWNED, WIDE + SIDE), 'cls', split_axis...]
  transfers between devices with their start and end apart: 1 -> 2, of which waited for: 1 -> 2; matrix products, arithmetic and copies ran while one was open for 2% -> 1% of each run, Pallas kernels for 0% -> 0%
where the time goes in v2:
time: 88.1 us; the launch traced here: 87.7 us
  waiting for transfers between devices  33.2 us (38%)
  starting transfers between devices  23.4 us (27%)
  blocking collectives  21.4 us (24%)
  Pallas kernels  8.95 us (10%)
    all_to_all x1, blocking collectives, body(): lax.all_to_all(averages, 'dom', split_axis=0, concat_axis=0, tiled=True)  21.4 us
    all_to_all x1, waiting for transfers between devices, body(): lax.all_to_all(payload, 'dom', split_axis=0, concat_axis=0, tiled=True)  18.4 us
    all_to_all x1, waiting for transfers between devices, body(): lax.all_to_all(sums.reshape(N_CLS, OWNED, WIDE + SIDE), 'cls', split_axis...  14.8 us
    all_to_all x1, starting transfers between devices, body(): lax.all_to_all(sums.reshape(N_CLS, OWNED, WIDE + SIDE), 'cls', split_axis...  12.9 us
    all_to_all x1, starting transfers between devices, body(): lax.all_to_all(payload, 'dom', split_axis=0, concat_axis=0, tiled=True)  10.5 us
    pallas_call x1, Pallas kernels, body(): pl.pallas_call(forward_kernel, out_shape=jax.ShapeDtypeStruct((N_DOM, ROW...  5.23 us
    pallas_call x1, Pallas kernels, body(): pl.pallas_call(invert_kernel, out_shape=jax.ShapeDtypeStruct((OWNED, SIDE...  2.14 us
  transfers between devices with their start and end apart: 2, of which 2 were waited for; matrix products, arithmetic and copies ran while one was open for 1% of the time, Pallas kernels for 0%

profile of v2, /device:TPU:1, one launch (start us, length us, event | category | flops | bytes accessed | tf_op | source)
XLA Modules:
  0.0 87.7 jit_solution(10706298115715330723)
XLA Ops:
  0.0 0.0 copy-start
  0.0 5.2 %shard_map.109 = bf16[32,144,128]{2,1,0:T(8,128)(2,1)} custom-call(s32[2,32]{1,0:T(2,128)} %bitcast.27, s32[32]{0:T(128)} %bins.1, s32[32]{0:T(128)} %class_ids.1, f32[32]{0:T(128)} %defocus.1, bf16[32,128,128]{2,1,0:T(8,128)(2,1)} %images.1, bf16[128,256]{1,0:T(8,128)(2,1)} %constant.25.clone.right, bf16[128,256]{1,0:T(8,128)(2,1)} %constant.26.clone.left), custom_call_target="tpu_custom_call" | custom-call | tf_op jit(solution)/shard_map/pallas_call | solution.py:254
  5.2 10.5 %all-to-all-start = ((bf16[32,144,128]{2,1,0:T(8,128)(2,1)}), bf16[32,144,128]{2,1,0:T(8,128)(2,1)S(1)}, u32[]{:S(2)}, u32[]{:S(2)}) async-start(bf16[32,144,128]{2,1,0:T(8,128)(2,1)} %shard_map.109), calls=%async_computation | async-start | bytes 2359296 | tf_op jit(solution)/shard_map/all_to_all | solution.py:269
  15.7 0.0 copy-start.3
  15.7 0.0 copy-start.4
  15.8 0.0 copy-start.5
  15.8 18.4 %all-to-all-done.arrived = bf16[32,144,128]{2,1,0:T(8,128)(2,1)S(1)} async-done(((bf16[32,144,128]{2,1,0:T(8,128)(2,1)}), bf16[32,144,128]{2,1,0:T(8,128)(2,1)S(1)}, u32[]{:S(2)}, u32[]{:S(2)}) %all-to-all-start) | async-done | bytes 1179680 | tf_op jit(solution)/shard_map/all_to_all | solution.py:269
  34.2 1.3 %shard_map.110 = bf16[256,640]{1,0:T(8,128)(2,1)} custom-call(bf16[32,144,128]{2,1,0:T(8,128)(2,1)S(1)} %all-to-all-done.arrived), custom_call_target="tpu_custom_call" | custom-call | tf_op jit(solution)/shard_map/pallas_call | solution.py:270
  35.5 12.9 %all-to-all-start.1 = ((bf16[16,16,640]{2,1,0:T(8,128)(2,1)}), bf16[16,16,640]{2,1,0:T(8,128)(2,1)S(1)}, u32[]{:S(2)}, u32[]{:S(2)}) async-start(bf16[16,16,640]{2,1,0:T(8,128)(2,1)} %bitcast.1), calls=%async_computation.1 | async-start | bytes 655360 | tf_op jit(solution)/shard_map/all_to_all | solution.py:278
  48.4 0.0 copy-done.3
  48.4 0.0 copy-done.4
  48.5 0.1 multiply_add_fusion
  48.6 0.1 copy.13
  48.7 0.1 copy.12
  48.8 0.0 copy-done.5
  48.8 0.1 multiply_cosine_fusion
  48.9 0.1 add_multiply_fusion
  49.1 0.0 copy-done
  49.1 0.0 copy-start.1
  49.2 0.0 copy-start.2
  49.2 14.8 %all-to-all-done.1.arrived = bf16[16,16,640]{2,1,0:T(8,128)(2,1)S(1)} async-done(((bf16[16,16,640]{2,1,0:T(8,128)(2,1)}), bf16[16,16,640]{2,1,0:T(8,128)(2,1)S(1)}, u32[]{:S(2)}, u32[]{:S(2)}) %all-to-all-start.1) | async-done | bytes 327712 | tf_op jit(solution)/shard_map/all_to_all | solution.py:278
  64.0 0.3 shard_map.111
  64.2 21.4 %all_to_all.15.arrived = bf16[32,64,128]{2,1,0:T(8,128)(2,1)S(1)} all-to-all(bf16[32,64,128]{2,1,0:T(8,128)(2,1)S(1)} %shard_map.111), channel_id=1, replica_groups=mesh['dom'=32,'cls'=16] {'dom'}, dimensions={0} | all-to-all | bytes 1048576 | tf_op jit(solution)/shard_map/all_to_all | solution.py:289
  85.6 2.1 %shard_map.112 = f32[16,128,128]{2,1,0:T(8,128)} custom-call(bf16[32,64,128]{2,1,0:T(8,128)(2,1)S(1)} %all_to_all.15.arrived, bf16[256,256]{1,0:T(8,128)(2,1)S(1)} %copy-done.1, bf16[256,128]{1,0:T(8,128)(2,1)S(1)} %copy-done.2), custom_call_target="tpu_custom_call" | custom-call | tf_op jit(solution)/shard_map/pallas_call | solution.py:291
  (7 shorter events, 0.1 us)
Async XLA Ops:
  0.0 49.1 %copy-start = (f32[128,128]{1,0:T(8,128)S(1)}, f32[128,128]{1,0:T(8,128)}, u32[]{:S(2)}) copy-start(f32[128,128]{1,0:T(8,128)} %param.16) | copy-start | bytes 196612
  5.2 28.9 %all-to-all-start = ((bf16[32,144,128]{2,1,0:T(8,128)(2,1)}), bf16[32,144,128]{2,1,0:T(8,128)(2,1)S(1)}, u32[]{:S(2)}, u32[]{:S(2)}) async-start(bf16[32,144,128]{2,1,0:T(8,128)(2,1)} %shard_map.109), calls=%async_computation | async-start | bytes 2359296 | tf_op jit(solution)/shard_map/all_to_all | solution.py:269
  15.7 32.7 %copy-start.3 = (f32[4,32]{0,1:T(8,128)S(1)}, f32[4,32]{0,1:T(8,128)}, u32[]{:S(2)}) copy-start(f32[4,32]{0,1:T(8,128)} %constant.33) | copy-start | bytes 1540
  15.7 32.7 %copy-start.4 = (f32[32]{0:T(128)S(1)}, f32[32]{0:T(128)}, u32[]{:S(2)}) copy-start(f32[32]{0:T(128)} %defocus.1) | copy-start | bytes 388
  15.8 33.0 %copy-start.5 = (f32[128]{0:T(128)S(1)}, f32[128]{0:T(128)}, u32[]{:S(2)}) copy-start(f32[128]{0:T(128)} %constant.24.clone) | copy-start | bytes 1540
  35.5 28.5 %all-to-all-start.1 = ((bf16[16,16,640]{2,1,0:T(8,128)(2,1)}), bf16[16,16,640]{2,1,0:T(8,128)(2,1)S(1)}, u32[]{:S(2)}, u32[]{:S(2)}) async-start(bf16[16,16,640]{2,1,0:T(8,128)(2,1)} %bitcast.1), calls=%async_computation.1 | async-start | bytes 655360 | tf_op jit(solution)/shard_map/all_to_all | solution.py:278
  49.1 36.4 %copy-start.1 = (bf16[256,256]{1,0:T(8,128)(2,1)S(1)}, bf16[256,256]{1,0:T(8,128)(2,1)}, u32[]{:S(2)}) copy-start(bf16[256,256]{1,0:T(8,128)(2,1)} %constant.27.clone.left) | copy-start | bytes 393220
  49.2 36.4 %copy-start.2 = (bf16[256,128]{1,0:T(8,128)(2,1)S(1)}, bf16[256,128]{1,0:T(8,128)(2,1)}, u32[]{:S(2)}) copy-start(bf16[256,128]{1,0:T(8,128)(2,1)} %constant.28.clone.right) | copy-start | bytes 196612

commit v3 on v2

--- a/solution.py
+++ b/solution.py
@@ -17,8 +17,13 @@
 N_CLS = 16
 BINS = 32
 REACH = 16
-PER = SIDE // N_DOM
-ROWS = PER * STACK + 16
+PAIR = 2
+TEAM = N_DOM * PAIR
+FAR = N_CLS // PAIR
+NEAR = OWNED * PAIR
+PER = SIDE // TEAM
+BLOCK = PER * STACK
+TAGS = 8
 WIDE = PER * SIDE
 GROUP = 16
 APART = SIDE + 8
@@ -60,6 +65,10 @@
     left = np.concatenate([left_high, left_low], axis=1)
     right_high, right_low = split(np.concatenate([cosine + sine, cosine - sine], axis=0))
     return left, right_high, right_low
+
+
+def member_index():
+    return lax.axis_index("dom") * PAIR + lax.rem(lax.axis_index("cls"), PAIR)
 
 
 def forward_kernel(
@@ -93,14 +102,14 @@
 
     tag_class = jnp.zeros((1, SIDE), jnp.int32)
     tag_bin = jnp.zeros((1, SIDE), jnp.int32)
-    first = lax.rem(lax.axis_index("dom"), 4) * STACK
+    first = lax.rem(member_index(), SIDE // STACK) * STACK
     for p in range(STACK):
         tag_class = jnp.where(lane[:1] == first + p, class_ids[p], tag_class)
         tag_bin = jnp.where(lane[:1] == first + p, bins[p], tag_bin)
-    tile = jnp.where(line[:16] == 0, tag_class, jnp.where(line[:16] == 1, tag_bin, 0))
+    tile = jnp.where(line[:TAGS] == 0, tag_class, jnp.where(line[:TAGS] == 1, tag_bin, 0))
     tile = tile.astype(jnp.float32).astype(jnp.bfloat16)
-    for d in range(N_DOM):
-        out[d, PER * STACK :, :] = tile
+    for m in range(TEAM):
+        out[m, BLOCK:, :] = tile
 
     def group(g, carry):
         picture_copy(g).wait()
@@ -142,9 +151,9 @@
 
     lax.fori_loop(0, STACK // GROUP, group, 0)
     for u in range(SIDE):
-        j, d = u // N_DOM, u % N_DOM
+        j, m = u // TEAM, u % TEAM
         row = spectra[pl.ds(u, STACK, stride=APART), :]
-        out[d, j * STACK : (j + 1) * STACK, :] = row.astype(jnp.bfloat16)
+        out[m, j * STACK : (j + 1) * STACK, :] = row.astype(jnp.bfloat16)
 
 
 def gather_kernel(arrived, out):
@@ -152,9 +161,9 @@
     classes = lax.broadcasted_iota(jnp.int32, (CLASSES, SIDE), 0).astype(jnp.float32)
     levels = (lax.broadcasted_iota(jnp.int32, (SIDE, SIDE), 0) % BINS).astype(jnp.float32)
     picks, lots, blocks = [], [], []
-    for g in range(N_DOM // together):
+    for g in range(TEAM // together):
         members = range(g * together, (g + 1) * together)
-        tag = sum(arrived[s, PER * STACK :, :].astype(jnp.float32) for s in members)
+        tag = sum(arrived[s, BLOCK:, :].astype(jnp.float32) for s in members)
         picks.append(jnp.where(classes == tag[0:1, :], 1.0, 0.0).astype(jnp.bfloat16))
         lots.append(jnp.where(levels == tag[1:2, :], 1.0, 0.0).astype(jnp.bfloat16))
         parts = [
@@ -170,41 +179,60 @@
         (((1,), (1,)), ((), ())),
         preferred_element_type=jnp.float32,
     )
-    lanes = lax.broadcasted_iota(jnp.int32, (CLASSES, SIDE), 1)
+    counts = counts.reshape(FAR, PAIR, OWNED, SIDE)
+    lanes = lax.broadcasted_iota(jnp.int32, (FAR, OWNED, SIDE), 2)
+    counts = jnp.where(lanes < SIDE // 2, counts[:, 0], counts[:, 1])
     high = jnp.floor(counts * (1.0 / 32.0))
     digits = jnp.where(lanes % (2 * BINS) < BINS, counts - 32.0 * high, high)
-    out[:, :WIDE] = sums.astype(jnp.bfloat16)
-    out[:, WIDE:] = digits.astype(jnp.bfloat16)
+    sums = sums.astype(jnp.bfloat16)
+    for j in range(PER):
+        out[:, j * NEAR : (j + 1) * NEAR, :] = sums[:, j * SIDE : (j + 1) * SIDE].reshape(
+            FAR, NEAR, SIDE
+        )
+    out[:, PER * NEAR :, :] = digits.astype(jnp.bfloat16)
 
 
 def average_kernel(arrived, squares, regular, out):
     total = arrived[0].astype(jnp.float32)
-    for z in range(1, N_CLS):
+    for z in range(1, FAR):
         total += arrived[z].astype(jnp.float32)
     lanes = lax.broadcasted_iota(jnp.int32, (OWNED, SIDE), 1)
     even = lanes % (2 * BINS) < BINS
-    digits = total[:, WIDE:]
+    digits = total[PER * NEAR :]
     ahead = pltpu.roll(digits, SIDE - BINS, axis=1)
     behind = pltpu.roll(digits, BINS, axis=1)
     counts = jnp.where(even, digits + 32.0 * ahead, behind + 32.0 * digits)
+    other = pltpu.roll(counts, SIDE // 2, axis=1)
+    near = lanes < SIDE // 2
+    counts = jnp.concatenate(
+        [jnp.where(near, counts, other), jnp.where(near, other, counts)], axis=0
+    )
+    even = jnp.concatenate([even, even], axis=0)
     high = jnp.floor(counts * (1.0 / 128.0))
     digits = jnp.where(even, counts - 128.0 * high, high).astype(jnp.bfloat16)
     denominator = jnp.dot(digits, squares[...], preferred_element_type=jnp.float32)
-    average = total[:, :WIDE] / (denominator + regular[...])
-    average = jnp.concatenate(
-        [average[:, j * SIDE : (j + 1) * SIDE] for j in range(PER)], axis=0
-    ).astype(jnp.bfloat16)
-    for d in range(N_DOM):
-        out[d] = average
+    denominator = denominator + regular[...]
+    averages = [
+        (
+            total[j * NEAR : (j + 1) * NEAR] / denominator[:, j * SIDE : (j + 1) * SIDE]
+        ).astype(jnp.bfloat16)
+        for j in range(PER)
+    ]
+    for i in range(PAIR):
+        block = jnp.concatenate(
+            [average[i * OWNED : (i + 1) * OWNED] for average in averages], axis=0
+        )
+        for d in range(N_DOM):
+            out[d * PAIR + i] = block
 
 
 def invert_kernel(arrived, left, right, out, rows):
     count = PER * OWNED
-    for d in range(N_DOM):
-        rows[d * SPREAD : d * SPREAD + count, :] = arrived[d].astype(jnp.float32)
+    for m in range(TEAM):
+        rows[m * SPREAD : m * SPREAD + count, :] = arrived[m].astype(jnp.float32)
 
     def picture(k):
-        parts = [rows[pl.ds(j * OWNED + k, N_DOM, stride=SPREAD), :] for j in range(PER)]
+        parts = [rows[pl.ds(j * OWNED + k, TEAM, stride=SPREAD), :] for j in range(PER)]
         return jnp.concatenate(parts, axis=0).astype(jnp.bfloat16)
 
     for k in range(0, OWNED, 2):
@@ -227,8 +255,20 @@
             out[k + i] = real * (1.0 / jnp.sqrt(power + EPSILON))
 
 
+TEAMS = [
+    [d * N_CLS + t * PAIR + i for d in range(N_DOM) for i in range(PAIR)] for t in range(FAR)
+]
+LINES = [[i + PAIR * t for t in range(FAR)] for i in range(PAIR)]
+
+
+def exchange(array, axes, groups):
+    return lax.all_to_all(
+        array, axes, split_axis=0, concat_axis=0, tiled=True, axis_index_groups=groups
+    )
+
+
 def body(images, class_ids, shifts, defocus_bins, defocus, regular):
-    dom = lax.axis_index("dom")
+    member = member_index()
     indices = np.arange(SIDE)
     signed = np.where(indices < SIDE // 2, indices, indices - SIDE).astype(np.float32) / SIDE
     squared = jnp.asarray((signed * signed).astype(np.float32))
@@ -238,7 +278,7 @@
 
     def own(table):
         return lax.dynamic_slice_in_dim(
-            table.reshape(*table.shape[:-1], PER, N_DOM), dom, 1, axis=-1
+            table.reshape(*table.shape[:-1], PER, TEAM), member, 1, axis=-1
         )
 
     mine = own(sin_u) * cos_v[:, None, :] + own(cos_u) * sin_v[:, None, :]
@@ -247,13 +287,13 @@
     low = (mine - high.astype(jnp.float32)).astype(jnp.bfloat16)
     squares = jnp.concatenate([high, 128 * high, low, 128 * low], axis=0)
     own_regular = lax.dynamic_slice_in_dim(
-        regular.reshape(PER, N_DOM, SIDE), dom, 1, axis=1
+        regular.reshape(PER, TEAM, SIDE), member, 1, axis=1
     ).reshape(1, WIDE)
 
     right, left = forward_tables()
     payload = pl.pallas_call(
         forward_kernel,
-        out_shape=jax.ShapeDtypeStruct((N_DOM, ROWS, SIDE), jnp.bfloat16),
+        out_shape=jax.ShapeDtypeStruct((TEAM, BLOCK + TAGS, SIDE), jnp.bfloat16),
         in_specs=[SMEM, SMEM, SMEM, SMEM, HBM, VMEM, VMEM],
         out_specs=VMEM,
         scratch_shapes=[
@@ -266,34 +306,32 @@
         compiler_params=ALL,
     )(shifts.T, defocus_bins, class_ids, defocus, images, jnp.asarray(right), jnp.asarray(left))
 
-    arrived = lax.all_to_all(payload, "dom", split_axis=0, concat_axis=0, tiled=True)
+    arrived = exchange(payload, ("dom", "cls"), TEAMS)
     sums = pl.pallas_call(
         gather_kernel,
-        out_shape=jax.ShapeDtypeStruct((CLASSES, WIDE + SIDE), jnp.bfloat16),
+        out_shape=jax.ShapeDtypeStruct((FAR, PER * NEAR + OWNED, SIDE), jnp.bfloat16),
         in_specs=[VMEM],
         out_specs=VMEM,
         compiler_params=PARAMS,
     )(arrived)
 
-    arrived = lax.all_to_all(
-        sums.reshape(N_CLS, OWNED, WIDE + SIDE), "cls", split_axis=0, concat_axis=0, tiled=True
-    )
+    arrived = exchange(sums, "cls", LINES)
     averages = pl.pallas_call(
         average_kernel,
-        out_shape=jax.ShapeDtypeStruct((N_DOM, PER * OWNED, SIDE), jnp.bfloat16),
+        out_shape=jax.ShapeDtypeStruct((TEAM, PER * OWNED, SIDE), jnp.bfloat16),
         in_specs=[VMEM, VMEM, VMEM],
         out_specs=VMEM,
         compiler_params=PARAMS,
     )(arrived, squares, own_regular)
 
-    arrived = lax.all_to_all(averages, "dom", split_axis=0, concat_axis=0, tiled=True)
+    arrived = exchange(averages, ("dom", "cls"), TEAMS)
     left, right, _ = inverse_tables()
     return pl.pallas_call(
         invert_kernel,
         out_shape=jax.ShapeDtypeStruct((OWNED, SIDE, SIDE), jnp.float32),
         in_specs=[VMEM, VMEM, VMEM],
         out_specs=VMEM,
-        scratch_shapes=[pltpu.VMEM((N_DOM * SPREAD, SIDE), jnp.float32)],
+        scratch_shapes=[pltpu.VMEM((TEAM * SPREAD, SIDE), jnp.float32)],
         compiler_params=PARAMS,
     )(arrived, jnp.asarray(left), jnp.asarray(right))
 

time: 88.1 us -> 87.2 us (0.990)
  waiting for transfers between devices: 33.2 us -> 30.9 us
  starting transfers between devices: 23.4 us -> 24.4 us
    all_to_all x2, waiting for transfers between devices: 33.2 us -> 30.9 us  [exchange(): lax.all_to_all(array, axes, split_axis=0, concat_axis=0, tiled=True, axis...]
    all_to_all x2, starting transfers between devices: 23.4 us -> 24.4 us  [exchange(): lax.all_to_all(array, axes, split_axis=0, concat_axis=0, tiled=True, axis...]
where the time goes in v3:
time: 87.2 us; the launch traced here: 86.8 us
  waiting for transfers between devices  30.9 us (35%)
  starting transfers between devices  24.4 us (28%)
  blocking collectives  21.1 us (24%)
  Pallas kernels  9.09 us (10%)
    all_to_all x2, waiting for transfers between devices, exchange(): lax.all_to_all(array, axes, split_axis=0, concat_axis=0, tiled=True, axis...  30.9 us
    all_to_all x2, starting transfers between devices, exchange(): lax.all_to_all(array, axes, split_axis=0, concat_axis=0, tiled=True, axis...  24.4 us
    all_to_all x1, blocking collectives, exchange(): lax.all_to_all(array, axes, split_axis=0, concat_axis=0, tiled=True, axis...  21.1 us
    pallas_call x1, Pallas kernels, body(): pl.pallas_call(forward_kernel, out_shape=jax.ShapeDtypeStruct((TEAM, BLOC...  5.24 us
    pallas_call x1, Pallas kernels, body(): pl.pallas_call(invert_kernel, out_shape=jax.ShapeDtypeStruct((OWNED, SIDE...  2.14 us
  transfers between devices with their start and end apart: 2, of which 2 were waited for; matrix products, arithmetic and copies ran while one was open for 1% of the time, Pallas kernels for 0%

profile of v3, /device:TPU:1, one launch (start us, length us, event | category | flops | bytes accessed | tf_op | source)
XLA Modules:
  0.0 86.8 jit_solution(13901920981830835606)
XLA Ops:
  0.0 0.0 copy-start
  0.0 5.2 %shard_map.109 = bf16[64,72,128]{2,1,0:T(8,128)(2,1)} custom-call(s32[2,32]{1,0:T(2,128)} %bitcast.26, s32[32]{0:T(128)} %bins.1, s32[32]{0:T(128)} %class_ids.1, f32[32]{0:T(128)} %defocus.1, bf16[32,128,128]{2,1,0:T(8,128)(2,1)} %images.1, bf16[128,256]{1,0:T(8,128)(2,1)} %constant.33.clone.right, bf16[128,256]{1,0:T(8,128)(2,1)} %constant.34.clone.left), custom_call_target="tpu_custom_call" | custom-call | tf_op jit(solution)/shard_map/pallas_call | solution.py:294
  5.3 0.0 copy-start.3
  5.3 0.0 copy-start.4
  5.3 0.0 copy-start.5
  5.3 11.1 %all-to-all-start = ((bf16[64,72,128]{2,1,0:T(8,128)(2,1)}), bf16[64,72,128]{2,1,0:T(8,128)(2,1)S(1)}, u32[]{:S(2)}, u32[]{:S(2)}) async-start(bf16[64,72,128]{2,1,0:T(8,128)(2,1)} %shard_map.109), calls=%async_computation | async-start | bytes 2359296 | tf_op jit(solution)/shard_map/all_to_all | solution.py:265
  16.4 0.0 copy-done.3
  16.4 0.0 copy-done.4
  16.4 0.1 multiply_add_fusion
  16.5 0.2 dynamic-slice_sine_fusion
  16.7 0.3 copy.22
  17.0 0.3 copy.21
  17.3 0.0 copy-done.5
  17.3 0.1 multiply_cosine_fusion
  17.5 17.7 %all-to-all-done.arrived = bf16[64,72,128]{2,1,0:T(8,128)(2,1)S(1)} async-done(((bf16[64,72,128]{2,1,0:T(8,128)(2,1)}), bf16[64,72,128]{2,1,0:T(8,128)(2,1)S(1)}, u32[]{:S(2)}, u32[]{:S(2)}) %all-to-all-start) | async-done | bytes 1179680 | tf_op jit(solution)/shard_map/all_to_all | solution.py:265
  35.2 1.4 %shard_map.110 = bf16[8,80,128]{2,1,0:T(8,128)(2,1)} custom-call(bf16[64,72,128]{2,1,0:T(8,128)(2,1)S(1)} %all-to-all-done.arrived), custom_call_target="tpu_custom_call" | custom-call | tf_op jit(solution)/shard_map/pallas_call | solution.py:310
  36.6 13.3 %all-to-all-start.1 = ((bf16[8,80,128]{2,1,0:T(8,128)(2,1)}), bf16[8,80,128]{2,1,0:T(8,128)(2,1)S(1)}, u32[]{:S(2)}, u32[]{:S(2)}) async-start(bf16[8,80,128]{2,1,0:T(8,128)(2,1)} %shard_map.110), calls=%async_computation.1 | async-start | bytes 327680 | tf_op jit(solution)/shard_map/all_to_all | solution.py:265
  49.9 0.1 add_multiply_fusion
  50.0 0.0 copy-done
  50.1 13.2 %all-to-all-done.1.arrived = bf16[8,80,128]{2,1,0:T(8,128)(2,1)S(1)} async-done(((bf16[8,80,128]{2,1,0:T(8,128)(2,1)}), bf16[8,80,128]{2,1,0:T(8,128)(2,1)S(1)}, u32[]{:S(2)}, u32[]{:S(2)}) %all-to-all-start.1) | async-done | bytes 163872 | tf_op jit(solution)/shard_map/all_to_all | solution.py:265
  63.3 0.3 shard_map.111
  63.6 21.1 %all_to_all.15.arrived = bf16[64,32,128]{2,1,0:T(8,128)(2,1)S(1)} all-to-all(bf16[64,32,128]{2,1,0:T(8,128)(2,1)S(1)} %shard_map.111), channel_id=1, replica_groups={{0,1,16,17,32,33,48,49,64,65,80,81,96,97,112,113,128,129,144,145,160,16..., dimensions={0} | all-to-all | bytes 1048576 | tf_op jit(solution)/shard_map/all_to_all | solution.py:265
  84.7 0.0 copy-done.2
  84.7 2.1 %shard_map.112 = f32[16,128,128]{2,1,0:T(8,128)} custom-call(bf16[64,32,128]{2,1,0:T(8,128)(2,1)S(1)} %all_to_all.15.arrived, bf16[256,256]{1,0:T(8,128)(2,1)S(1)} %copy-done.1, bf16[256,128]{1,0:T(8,128)(2,1)S(1)} %copy-done.2), custom_call_target="tpu_custom_call" | custom-call | tf_op jit(solution)/shard_map/pallas_call | solution.py:329
  (7 shorter events, 0.0 us)
Async XLA Ops:
  0.0 50.0 %copy-start = (f32[128,128]{1,0:T(8,128)S(1)}, f32[128,128]{1,0:T(8,128)}, u32[]{:S(2)}) copy-start(f32[128,128]{1,0:T(8,128)} %param.16) | copy-start | bytes 196612
  5.3 11.2 %copy-start.3 = (f32[32]{0:T(128)S(1)}, f32[32]{0:T(128)}, u32[]{:S(2)}) copy-start(f32[32]{0:T(128)} %defocus.1) | copy-start | bytes 388
  5.3 11.2 %copy-start.4 = (f32[2,64]{1,0:T(2,128)S(1)}, f32[2,64]{1,0:T(2,128)}, u32[]{:S(2)}) copy-start(f32[2,64]{1,0:T(2,128)} %constant.41) | copy-start | bytes 1540
  5.3 12.1 %copy-start.5 = (f32[128]{0:T(128)S(1)}, f32[128]{0:T(128)}, u32[]{:S(2)}) copy-start(f32[128]{0:T(128)} %constant.32.clone) | copy-start | bytes 1540
  5.3 29.9 %all-to-all-start = ((bf16[64,72,128]{2,1,0:T(8,128)(2,1)}), bf16[64,72,128]{2,1,0:T(8,128)(2,1)S(1)}, u32[]{:S(2)}, u32[]{:S(2)}) async-start(bf16[64,72,128]{2,1,0:T(8,128)(2,1)} %shard_map.109), calls=%async_computation | async-start | bytes 2359296 | tf_op jit(solution)/shard_map/all_to_all | solution.py:265
  36.6 48.2 %copy-start.1 = (bf16[256,256]{1,0:T(8,128)(2,1)S(1)}, bf16[256,256]{1,0:T(8,128)(2,1)}, u32[]{:S(2)}) copy-start(bf16[256,256]{1,0:T(8,128)(2,1)} %constant.35.clone.left) | copy-start | bytes 393220
  36.6 48.2 %copy-start.2 = (bf16[256,128]{1,0:T(8,128)(2,1)S(1)}, bf16[256,128]{1,0:T(8,128)(2,1)}, u32[]{:S(2)}) copy-start(bf16[256,128]{1,0:T(8,128)(2,1)} %constant.36.clone.right) | copy-start | bytes 196612
  36.6 26.7 %all-to-all-start.1 = ((bf16[8,80,128]{2,1,0:T(8,128)(2,1)}), bf16[8,80,128]{2,1,0:T(8,128)(2,1)S(1)}, u32[]{:S(2)}, u32[]{:S(2)}) async-start(bf16[8,80,128]{2,1,0:T(8,128)(2,1)} %shard_map.110), calls=%async_computation.1 | async-start | bytes 327680 | tf_op jit(solution)/shard_map/all_to_all | solution.py:265

commit v4 on v3

--- a/solution.py
+++ b/solution.py
@@ -24,6 +24,8 @@
 PER = SIDE // TEAM
 BLOCK = PER * STACK
 TAGS = 8
+TURN = 5
+START = 21
 WIDE = PER * SIDE
 GROUP = 16
 APART = SIDE + 8
@@ -68,7 +70,7 @@
 
 
 def member_index():
-    return lax.axis_index("dom") * PAIR + lax.rem(lax.axis_index("cls"), PAIR)
+    return lax.rem(lax.axis_index("dom") + N_DOM - START, N_DOM) * PAIR + lax.rem(lax.axis_index("cls"), PAIR)
 
 
 def forward_kernel(
@@ -185,11 +187,14 @@
     high = jnp.floor(counts * (1.0 / 32.0))
     digits = jnp.where(lanes % (2 * BINS) < BINS, counts - 32.0 * high, high)
     sums = sums.astype(jnp.bfloat16)
-    for j in range(PER):
-        out[:, j * NEAR : (j + 1) * NEAR, :] = sums[:, j * SIDE : (j + 1) * SIDE].reshape(
-            FAR, NEAR, SIDE
-        )
-    out[:, PER * NEAR :, :] = digits.astype(jnp.bfloat16)
+    digits = digits.astype(jnp.bfloat16)
+    for t in range(FAR):
+        far = (t + TURN) % FAR
+        for j in range(PER):
+            out[t, j * NEAR : (j + 1) * NEAR, :] = sums[
+                far * NEAR : (far + 1) * NEAR, j * SIDE : (j + 1) * SIDE
+            ]
+        out[t, PER * NEAR :, :] = digits[far]
 
 
 def average_kernel(arrived, squares, regular, out):
@@ -256,9 +261,12 @@
 
 
 TEAMS = [
-    [d * N_CLS + t * PAIR + i for d in range(N_DOM) for i in range(PAIR)] for t in range(FAR)
+    [
+        (d + START) % N_DOM * N_CLS + t * PAIR + i for d in range(N_DOM) for i in range(PAIR)
+    ]
+    for t in range(FAR)
 ]
-LINES = [[i + PAIR * t for t in range(FAR)] for i in range(PAIR)]
+LINES = [[i + PAIR * ((t + TURN) % FAR) for t in range(FAR)] for i in range(PAIR)]
 
 
 def exchange(array, axes, groups):

time: 87.2 us -> 77 us (0.88)
  waiting for transfers between devices: 30.9 us -> 22 us
  blocking collectives: 21.1 us -> 17.1 us
  starting transfers between devices: 24.4 us -> 27.1 us
    all_to_all x2, waiting for transfers between devices: 30.9 us -> 22 us  [exchange(): lax.all_to_all(array, axes, split_axis=0, concat_axis=0, tiled=True, axis...]
    all_to_all x1, blocking collectives: 21.1 us -> 17.1 us  [exchange(): lax.all_to_all(array, axes, split_axis=0, concat_axis=0, tiled=True, axis...]
    all_to_all x2, starting transfers between devices: 24.4 us -> 27.1 us  [exchange(): lax.all_to_all(array, axes, split_axis=0, concat_axis=0, tiled=True, axis...]
  transfers between devices with their start and end apart: 2 -> 2, of which waited for: 2 -> 2; matrix products, arithmetic and copies ran while one was open for 1% -> 2% of each run, Pallas kernels for 0% -> 0%
where the time goes in v4:
time: 77 us; the launch traced here: 76.6 us
  starting transfers between devices  27.1 us (35%)
  waiting for transfers between devices  22 us (29%)
  blocking collectives  17.1 us (22%)
  Pallas kernels  9.1 us (12%)
  local copies, waits for them, and re-layouts  0.85 us (1%)
    all_to_all x2, starting transfers between devices, exchange(): lax.all_to_all(array, axes, split_axis=0, concat_axis=0, tiled=True, axis...  27.1 us
    all_to_all x2, waiting for transfers between devices, exchange(): lax.all_to_all(array, axes, split_axis=0, concat_axis=0, tiled=True, axis...  22 us
    all_to_all x1, blocking collectives, exchange(): lax.all_to_all(array, axes, split_axis=0, concat_axis=0, tiled=True, axis...  17.1 us
    pallas_call x1, Pallas kernels, body(): pl.pallas_call(forward_kernel, out_shape=jax.ShapeDtypeStruct((TEAM, BLOC...  5.24 us
    pallas_call x1, Pallas kernels, body(): pl.pallas_call(invert_kernel, out_shape=jax.ShapeDtypeStruct((OWNED, SIDE...  2.14 us
  transfers between devices with their start and end apart: 2, of which 2 were waited for; matrix products, arithmetic and copies ran while one was open for 2% of the time, Pallas kernels for 0%

profile of v4, /device:TPU:1, one launch (start us, length us, event | category | flops | bytes accessed | tf_op | source)
XLA Modules:
  0.0 76.6 jit_solution(4468849308449663036)
XLA Ops:
  0.0 0.0 copy-start
  0.0 5.2 %shard_map.109 = bf16[64,72,128]{2,1,0:T(8,128)(2,1)} custom-call(s32[2,32]{1,0:T(2,128)} %bitcast.26, s32[32]{0:T(128)} %bins.1, s32[32]{0:T(128)} %class_ids.1, f32[32]{0:T(128)} %defocus.1, bf16[32,128,128]{2,1,0:T(8,128)(2,1)} %images.1, bf16[128,256]{1,0:T(8,128)(2,1)} %constant.41.clone.right, bf16[128,256]{1,0:T(8,128)(2,1)} %constant.42.clone.left), custom_call_target="tpu_custom_call" | custom-call | tf_op jit(solution)/shard_map/pallas_call | solution.py:302
  5.3 0.0 copy-start.3
  5.3 0.0 copy-start.4
  5.3 0.0 copy-start.5
  5.3 14.2 %all-to-all-start = ((bf16[64,72,128]{2,1,0:T(8,128)(2,1)}), bf16[64,72,128]{2,1,0:T(8,128)(2,1)S(1)}, u32[]{:S(2)}, u32[]{:S(2)}) async-start(bf16[64,72,128]{2,1,0:T(8,128)(2,1)} %shard_map.109), calls=%async_computation | async-start | bytes 2359296 | tf_op jit(solution)/shard_map/all_to_all | solution.py:273
  19.5 0.0 copy-done.3
  19.5 0.0 copy-done.4
  19.5 0.1 multiply_add_fusion
  19.6 0.2 dynamic-slice_sine_fusion
  19.8 0.3 copy.22
  20.1 0.3 copy.21
  20.4 0.0 copy-done.5
  20.4 0.1 multiply_cosine_fusion
  20.5 13.7 %all-to-all-done.arrived = bf16[64,72,128]{2,1,0:T(8,128)(2,1)S(1)} async-done(((bf16[64,72,128]{2,1,0:T(8,128)(2,1)}), bf16[64,72,128]{2,1,0:T(8,128)(2,1)S(1)}, u32[]{:S(2)}, u32[]{:S(2)}) %all-to-all-start) | async-done | bytes 1179680 | tf_op jit(solution)/shard_map/all_to_all | solution.py:273
  34.2 1.4 %shard_map.110 = bf16[8,80,128]{2,1,0:T(8,128)(2,1)} custom-call(bf16[64,72,128]{2,1,0:T(8,128)(2,1)S(1)} %all-to-all-done.arrived), custom_call_target="tpu_custom_call" | custom-call | tf_op jit(solution)/shard_map/pallas_call | solution.py:318
  35.6 12.9 %all-to-all-start.1 = ((bf16[8,80,128]{2,1,0:T(8,128)(2,1)}), bf16[8,80,128]{2,1,0:T(8,128)(2,1)S(1)}, u32[]{:S(2)}, u32[]{:S(2)}) async-start(bf16[8,80,128]{2,1,0:T(8,128)(2,1)} %shard_map.110), calls=%async_computation.1 | async-start | bytes 327680 | tf_op jit(solution)/shard_map/all_to_all | solution.py:273
  48.5 0.1 add_multiply_fusion
  48.6 0.0 copy-done
  48.7 8.3 %all-to-all-done.1.arrived = bf16[8,80,128]{2,1,0:T(8,128)(2,1)S(1)} async-done(((bf16[8,80,128]{2,1,0:T(8,128)(2,1)}), bf16[8,80,128]{2,1,0:T(8,128)(2,1)S(1)}, u32[]{:S(2)}, u32[]{:S(2)}) %all-to-all-start.1) | async-done | bytes 163872 | tf_op jit(solution)/shard_map/all_to_all | solution.py:273
  57.0 0.3 shard_map.111
  57.4 17.1 %all_to_all.15.arrived = bf16[64,32,128]{2,1,0:T(8,128)(2,1)S(1)} all-to-all(bf16[64,32,128]{2,1,0:T(8,128)(2,1)S(1)} %shard_map.111), channel_id=1, replica_groups={{336,337,352,353,368,369,384,385,400,401,416,417,432,433,448,449,464,46..., dimensions={0} | all-to-all | bytes 1048576 | tf_op jit(solution)/shard_map/all_to_all | solution.py:273
  74.5 0.0 copy-done.2
  74.5 2.1 %shard_map.112 = f32[16,128,128]{2,1,0:T(8,128)} custom-call(bf16[64,32,128]{2,1,0:T(8,128)(2,1)S(1)} %all_to_all.15.arrived, bf16[256,256]{1,0:T(8,128)(2,1)S(1)} %copy-done.1, bf16[256,128]{1,0:T(8,128)(2,1)S(1)} %copy-done.2), custom_call_target="tpu_custom_call" | custom-call | tf_op jit(solution)/shard_map/pallas_call | solution.py:337
  (7 shorter events, 0.0 us)
Async XLA Ops:
  0.0 48.6 %copy-start = (f32[128,128]{1,0:T(8,128)S(1)}, f32[128,128]{1,0:T(8,128)}, u32[]{:S(2)}) copy-start(f32[128,128]{1,0:T(8,128)} %param.16) | copy-start | bytes 196612
  5.3 14.2 %copy-start.3 = (f32[32]{0:T(128)S(1)}, f32[32]{0:T(128)}, u32[]{:S(2)}) copy-start(f32[32]{0:T(128)} %defocus.1) | copy-start | bytes 388
  5.3 14.2 %copy-start.4 = (f32[2,64]{1,0:T(2,128)S(1)}, f32[2,64]{1,0:T(2,128)}, u32[]{:S(2)}) copy-start(f32[2,64]{1,0:T(2,128)} %constant.49) | copy-start | bytes 1540
  5.3 15.1 %copy-start.5 = (f32[128]{0:T(128)S(1)}, f32[128]{0:T(128)}, u32[]{:S(2)}) copy-start(f32[128]{0:T(128)} %constant.40.clone) | copy-start | bytes 1540
  5.3 28.9 %all-to-all-start = ((bf16[64,72,128]{2,1,0:T(8,128)(2,1)}), bf16[64,72,128]{2,1,0:T(8,128)(2,1)S(1)}, u32[]{:S(2)}, u32[]{:S(2)}) async-start(bf16[64,72,128]{2,1,0:T(8,128)(2,1)} %shard_map.109), calls=%async_computation | async-start | bytes 2359296 | tf_op jit(solution)/shard_map/all_to_all | solution.py:273
  35.6 38.9 %copy-start.1 = (bf16[256,256]{1,0:T(8,128)(2,1)S(1)}, bf16[256,256]{1,0:T(8,128)(2,1)}, u32[]{:S(2)}) copy-start(bf16[256,256]{1,0:T(8,128)(2,1)} %constant.43.clone.left) | copy-start | bytes 393220
  35.6 38.9 %copy-start.2 = (bf16[256,128]{1,0:T(8,128)(2,1)S(1)}, bf16[256,128]{1,0:T(8,128)(2,1)}, u32[]{:S(2)}) copy-start(bf16[256,128]{1,0:T(8,128)(2,1)} %constant.44.clone.right) | copy-start | bytes 196612
  35.6 21.4 %all-to-all-start.1 = ((bf16[8,80,128]{2,1,0:T(8,128)(2,1)}), bf16[8,80,128]{2,1,0:T(8,128)(2,1)S(1)}, u32[]{:S(2)}, u32[]{:S(2)}) async-start(bf16[8,80,128]{2,1,0:T(8,128)(2,1)} %shard_map.110), calls=%async_computation.1 | async-start | bytes 327680 | tf_op jit(solution)/shard_map/all_to_all | solution.py:273

commit v5 on v4

--- a/solution.py
+++ b/solution.py
@@ -24,10 +24,12 @@
 PER = SIDE // TEAM
 BLOCK = PER * STACK
 TAGS = 8
-TURN = 5
+ORDER = (5, 1, 6, 2, 7, 3, 0, 4)
 START = 21
+LAST = 21
 WIDE = PER * SIDE
 GROUP = 16
+SLAB = 16
 APART = SIDE + 8
 SPREAD = PER * OWNED + 8
 PHASE = 0.1
@@ -74,7 +76,7 @@
 
 
 def forward_kernel(
-    shifts, bins, class_ids, defocus, images, right, left, out, pictures, moved, spectra, trig, sems
+    shifts, bins, class_ids, defocus, images, right, left, sent, out, pictures, moved, spectra, trig, sems, out_sems
 ):
     def picture_copy(g):
         part = pl.ds(g * GROUP, GROUP)
@@ -152,10 +154,18 @@
         return carry
 
     lax.fori_loop(0, STACK // GROUP, group, 0)
-    for u in range(SIDE):
-        j, m = u // TEAM, u % TEAM
-        row = spectra[pl.ds(u, STACK, stride=APART), :]
-        out[m, j * STACK : (j + 1) * STACK, :] = row.astype(jnp.bfloat16)
+    def sent_copy(c):
+        part = pl.ds(c * SLAB, SLAB)
+        return pltpu.make_async_copy(out.at[part], sent.at[part], out_sems.at[c])
+
+    for c in range(TEAM // SLAB):
+        for m in range(c * SLAB, (c + 1) * SLAB):
+            for j in range(PER):
+                row = spectra[pl.ds(j * TEAM + m, STACK, stride=APART), :]
+                out[m, j * STACK : (j + 1) * STACK, :] = row.astype(jnp.bfloat16)
+        sent_copy(c).start()
+    for c in range(TEAM // SLAB):
+        sent_copy(c).wait()
 
 
 def gather_kernel(arrived, out):
@@ -189,7 +199,7 @@
     sums = sums.astype(jnp.bfloat16)
     digits = digits.astype(jnp.bfloat16)
     for t in range(FAR):
-        far = (t + TURN) % FAR
+        far = ORDER[t]
         for j in range(PER):
             out[t, j * NEAR : (j + 1) * NEAR, :] = sums[
                 far * NEAR : (far + 1) * NEAR, j * SIDE : (j + 1) * SIDE
@@ -231,14 +241,19 @@
             out[d * PAIR + i] = block
 
 
-def invert_kernel(arrived, left, right, out, rows):
+def invert_kernel(arrived, left, right, result, out, rows, sems):
     count = PER * OWNED
-    for m in range(TEAM):
-        rows[m * SPREAD : m * SPREAD + count, :] = arrived[m].astype(jnp.float32)
+    for q in range(TEAM):
+        m = (q + (LAST - START) * PAIR) % TEAM
+        rows[m * SPREAD : m * SPREAD + count, :] = arrived[q].astype(jnp.float32)
 
     def picture(k):
         parts = [rows[pl.ds(j * OWNED + k, TEAM, stride=SPREAD), :] for j in range(PER)]
         return jnp.concatenate(parts, axis=0).astype(jnp.bfloat16)
+
+    def result_copy(k):
+        part = pl.ds(k, 2)
+        return pltpu.make_async_copy(out.at[part], result.at[part], sems.at[k // 2])
 
     for k in range(0, OWNED, 2):
         both = jnp.concatenate([picture(k), picture(k + 1)], axis=1)
@@ -258,15 +273,19 @@
             power = jnp.sum(real * real, axis=0, keepdims=True)
             power = jnp.sum(power, axis=1, keepdims=True) * (1.0 / (SIDE * SIDE))
             out[k + i] = real * (1.0 / jnp.sqrt(power + EPSILON))
-
-
-TEAMS = [
-    [
-        (d + START) % N_DOM * N_CLS + t * PAIR + i for d in range(N_DOM) for i in range(PAIR)
+        result_copy(k).start()
+    for k in range(0, OWNED, 2):
+        result_copy(k).wait()
+
+
+def teams(start):
+    return [
+        [(d + start) % N_DOM * N_CLS + t * PAIR + i for d in range(N_DOM) for i in range(PAIR)]
+        for t in range(FAR)
     ]
-    for t in range(FAR)
-]
-LINES = [[i + PAIR * ((t + TURN) % FAR) for t in range(FAR)] for i in range(PAIR)]
+
+
+LINES = [[i + PAIR * t for t in ORDER] for i in range(PAIR)]
 
 
 def exchange(array, axes, groups):
@@ -303,18 +322,20 @@
         forward_kernel,
         out_shape=jax.ShapeDtypeStruct((TEAM, BLOCK + TAGS, SIDE), jnp.bfloat16),
         in_specs=[SMEM, SMEM, SMEM, SMEM, HBM, VMEM, VMEM],
-        out_specs=VMEM,
+        out_specs=HBM,
         scratch_shapes=[
+            pltpu.VMEM((TEAM, BLOCK + TAGS, SIDE), jnp.bfloat16),
             pltpu.VMEM((STACK, SIDE, SIDE), jnp.bfloat16),
             pltpu.VMEM((GROUP, SIDE + 2 * REACH, SIDE), jnp.float32),
-            pltpu.VMEM((STACK * APART, SIDE), jnp.float32),
+            pltpu.VMEM(((STACK + 1) * APART, SIDE), jnp.float32),
             pltpu.VMEM((2, SIDE + BINS, SIDE), jnp.float32),
             pltpu.SemaphoreType.DMA((STACK // GROUP,)),
+            pltpu.SemaphoreType.DMA((TEAM // SLAB,)),
         ],
         compiler_params=ALL,
     )(shifts.T, defocus_bins, class_ids, defocus, images, jnp.asarray(right), jnp.asarray(left))
 
-    arrived = exchange(payload, ("dom", "cls"), TEAMS)
+    arrived = exchange(payload, ("dom", "cls"), teams(START))
     sums = pl.pallas_call(
         gather_kernel,
         out_shape=jax.ShapeDtypeStruct((FAR, PER * NEAR + OWNED, SIDE), jnp.bfloat16),
@@ -332,14 +353,18 @@
         compiler_params=PARAMS,
     )(arrived, squares, own_regular)
 
-    arrived = exchange(averages, ("dom", "cls"), TEAMS)
+    arrived = exchange(averages, ("dom", "cls"), teams(LAST))
     left, right, _ = inverse_tables()
     return pl.pallas_call(
         invert_kernel,
         out_shape=jax.ShapeDtypeStruct((OWNED, SIDE, SIDE), jnp.float32),
         in_specs=[VMEM, VMEM, VMEM],
-        out_specs=VMEM,
-        scratch_shapes=[pltpu.VMEM((TEAM * SPREAD, SIDE), jnp.float32)],
+        out_specs=HBM,
+        scratch_shapes=[
+            pltpu.VMEM((OWNED, SIDE, SIDE), jnp.float32),
+            pltpu.VMEM(((TEAM + 1) * SPREAD, SIDE), jnp.float32),
+            pltpu.SemaphoreType.DMA((OWNED // 2,)),
+        ],
         compiler_params=PARAMS,
     )(arrived, jnp.asarray(left), jnp.asarray(right))
 

time: 77 us -> 76.3 us (level)
  no operation moved by 1% of the time
where the time goes in v5:
time: 76.3 us; the launch traced here: 75.9 us
  starting transfers between devices  27 us (35%)
  waiting for transfers between devices  21.4 us (28%)
  blocking collectives  17.5 us (23%)
  Pallas kernels  8.62 us (11%)
  local copies, waits for them, and re-layouts  0.85 us (1%)
    all_to_all x2, starting transfers between devices, exchange(): lax.all_to_all(array, axes, split_axis=0, concat_axis=0, tiled=True, axis...  27 us
    all_to_all x2, waiting for transfers between devices, exchange(): lax.all_to_all(array, axes, split_axis=0, concat_axis=0, tiled=True, axis...  21.4 us
    all_to_all x1, blocking collectives, exchange(): lax.all_to_all(array, axes, split_axis=0, concat_axis=0, tiled=True, axis...  17.5 us
    pallas_call x1, Pallas kernels, body(): pl.pallas_call(forward_kernel, out_shape=jax.ShapeDtypeStruct((TEAM, BLOC...  5.02 us
    pallas_call x1, Pallas kernels, body(): pl.pallas_call(invert_kernel, out_shape=jax.ShapeDtypeStruct((OWNED, SIDE...  1.89 us
  transfers between devices with their start and end apart: 2, of which 2 were waited for; matrix products, arithmetic and copies ran while one was open for 2% of the time, Pallas kernels for 0%

profile of v5, /device:TPU:1, one launch (start us, length us, event | category | flops | bytes accessed | tf_op | source)
XLA Modules:
  0.0 75.9 jit_solution(18245087017462173383)
XLA Ops:
  0.0 0.0 copy-start
  0.0 5.0 %shard_map.109 = bf16[64,72,128]{2,1,0:T(8,128)(2,1)} custom-call(s32[2,32]{1,0:T(2,128)} %bitcast.26, s32[32]{0:T(128)} %bins.1, s32[32]{0:T(128)} %class_ids.1, f32[32]{0:T(128)} %defocus.1, bf16[32,128,128]{2,1,0:T(8,128)(2,1)} %images.1, bf16[128,256]{1,0:T(8,128)(2,1)} %constant.41.clone.right, bf16[128,256]{1,0:T(8,128)(2,1)} %constant.42.clone.left), custom_call_target="tpu_custom_call" | custom-call | tf_op jit(solution)/shard_map/pallas_call | solution.py:321
  5.0 0.0 copy-start.3
  5.0 0.0 copy-start.4
  5.1 0.0 copy-start.5
  5.1 14.2 %all-to-all-start = ((bf16[64,72,128]{2,1,0:T(8,128)(2,1)}), bf16[64,72,128]{2,1,0:T(8,128)(2,1)S(1)}, u32[]{:S(2)}, u32[]{:S(2)}) async-start(bf16[64,72,128]{2,1,0:T(8,128)(2,1)} %shard_map.109), calls=%async_computation | async-start | bytes 2359296 | tf_op jit(solution)/shard_map/all_to_all | solution.py:292
  19.3 0.0 copy-done.3
  19.3 0.0 copy-done.4
  19.3 0.1 multiply_add_fusion
  19.4 0.2 dynamic-slice_sine_fusion
  19.6 0.3 copy.22
  19.9 0.3 copy.21
  20.2 0.0 copy-done.5
  20.2 0.1 multiply_cosine_fusion
  20.3 13.7 %all-to-all-done.arrived = bf16[64,72,128]{2,1,0:T(8,128)(2,1)S(1)} async-done(((bf16[64,72,128]{2,1,0:T(8,128)(2,1)}), bf16[64,72,128]{2,1,0:T(8,128)(2,1)S(1)}, u32[]{:S(2)}, u32[]{:S(2)}) %all-to-all-start) | async-done | bytes 1179680 | tf_op jit(solution)/shard_map/all_to_all | solution.py:292
  34.0 1.4 %shard_map.110 = bf16[8,80,128]{2,1,0:T(8,128)(2,1)} custom-call(bf16[64,72,128]{2,1,0:T(8,128)(2,1)S(1)} %all-to-all-done.arrived), custom_call_target="tpu_custom_call" | custom-call | tf_op jit(solution)/shard_map/pallas_call | solution.py:339
  35.4 12.9 %all-to-all-start.1 = ((bf16[8,80,128]{2,1,0:T(8,128)(2,1)}), bf16[8,80,128]{2,1,0:T(8,128)(2,1)S(1)}, u32[]{:S(2)}, u32[]{:S(2)}) async-start(bf16[8,80,128]{2,1,0:T(8,128)(2,1)} %shard_map.110), calls=%async_computation.1 | async-start | bytes 327680 | tf_op jit(solution)/shard_map/all_to_all | solution.py:292
  48.3 0.1 add_multiply_fusion
  48.4 0.0 copy-done
  48.5 7.8 %all-to-all-done.1.arrived = bf16[8,80,128]{2,1,0:T(8,128)(2,1)S(1)} async-done(((bf16[8,80,128]{2,1,0:T(8,128)(2,1)}), bf16[8,80,128]{2,1,0:T(8,128)(2,1)S(1)}, u32[]{:S(2)}, u32[]{:S(2)}) %all-to-all-start.1) | async-done | bytes 163872 | tf_op jit(solution)/shard_map/all_to_all | solution.py:292
  56.2 0.3 shard_map.111
  56.6 17.5 %all_to_all.15.arrived = bf16[64,32,128]{2,1,0:T(8,128)(2,1)S(1)} all-to-all(bf16[64,32,128]{2,1,0:T(8,128)(2,1)S(1)} %shard_map.111), channel_id=1, replica_groups={{336,337,352,353,368,369,384,385,400,401,416,417,432,433,448,449,464,46..., dimensions={0} | all-to-all | bytes 1048576 | tf_op jit(solution)/shard_map/all_to_all | solution.py:292
  74.0 0.0 copy-done.2
  74.0 1.9 %shard_map.112 = f32[16,128,128]{2,1,0:T(8,128)} custom-call(bf16[64,32,128]{2,1,0:T(8,128)(2,1)S(1)} %all_to_all.15.arrived, bf16[256,256]{1,0:T(8,128)(2,1)S(1)} %copy-done.1, bf16[256,128]{1,0:T(8,128)(2,1)S(1)} %copy-done.2), custom_call_target="tpu_custom_call" | custom-call | tf_op jit(solution)/shard_map/pallas_call | solution.py:358
  (7 shorter events, 0.0 us)
Async XLA Ops:
  0.0 48.4 %copy-start = (f32[128,128]{1,0:T(8,128)S(1)}, f32[128,128]{1,0:T(8,128)}, u32[]{:S(2)}) copy-start(f32[128,128]{1,0:T(8,128)} %param.16) | copy-start | bytes 196612
  5.0 14.2 %copy-start.3 = (f32[32]{0:T(128)S(1)}, f32[32]{0:T(128)}, u32[]{:S(2)}) copy-start(f32[32]{0:T(128)} %defocus.1) | copy-start | bytes 388
  5.0 14.2 %copy-start.4 = (f32[2,64]{1,0:T(2,128)S(1)}, f32[2,64]{1,0:T(2,128)}, u32[]{:S(2)}) copy-start(f32[2,64]{1,0:T(2,128)} %constant.49) | copy-start | bytes 1540
  5.1 15.1 %copy-start.5 = (f32[128]{0:T(128)S(1)}, f32[128]{0:T(128)}, u32[]{:S(2)}) copy-start(f32[128]{0:T(128)} %constant.40.clone) | copy-start | bytes 1540
  5.1 28.9 %all-to-all-start = ((bf16[64,72,128]{2,1,0:T(8,128)(2,1)}), bf16[64,72,128]{2,1,0:T(8,128)(2,1)S(1)}, u32[]{:S(2)}, u32[]{:S(2)}) async-start(bf16[64,72,128]{2,1,0:T(8,128)(2,1)} %shard_map.109), calls=%async_computation | async-start | bytes 2359296 | tf_op jit(solution)/shard_map/all_to_all | solution.py:292
  35.4 38.6 %copy-start.1 = (bf16[256,256]{1,0:T(8,128)(2,1)S(1)}, bf16[256,256]{1,0:T(8,128)(2,1)}, u32[]{:S(2)}) copy-start(bf16[256,256]{1,0:T(8,128)(2,1)} %constant.43.clone.left) | copy-start | bytes 393220
  35.4 38.6 %copy-start.2 = (bf16[256,128]{1,0:T(8,128)(2,1)S(1)}, bf16[256,128]{1,0:T(8,128)(2,1)}, u32[]{:S(2)}) copy-start(bf16[256,128]{1,0:T(8,128)(2,1)} %constant.44.clone.right) | copy-start | bytes 196612
  35.4 20.8 %all-to-all-start.1 = ((bf16[8,80,128]{2,1,0:T(8,128)(2,1)}), bf16[8,80,128]{2,1,0:T(8,128)(2,1)S(1)}, u32[]{:S(2)}, u32[]{:S(2)}) async-start(bf16[8,80,128]{2,1,0:T(8,128)(2,1)} %shard_map.110), calls=%async_computation.1 | async-start | bytes 327680 | tf_op jit(solution)/shard_map/all_to_all | solution.py:292

commit v6 on v5

--- a/solution.py
+++ b/solution.py
@@ -25,11 +25,13 @@
 BLOCK = PER * STACK
 TAGS = 8
 ORDER = (5, 1, 6, 2, 7, 3, 0, 4)
-START = 21
-LAST = 21
+STRIDE = 13
+FOLD = 4
+HEAD = 42
 WIDE = PER * SIDE
 GROUP = 16
-SLAB = 16
+SLAB = 8
+LOT = 8
 APART = SIDE + 8
 SPREAD = PER * OWNED + 8
 PHASE = 0.1
@@ -71,19 +73,40 @@
     return left, right_high, right_low
 
 
+def place(device):
+    mixed = (device * STRIDE + (TEAM - HEAD) * STRIDE) % TEAM
+    return mixed ^ (mixed // FOLD)
+
+
 def member_index():
-    return lax.rem(lax.axis_index("dom") + N_DOM - START, N_DOM) * PAIR + lax.rem(lax.axis_index("cls"), PAIR)
+    return place(lax.axis_index("dom") * PAIR + lax.rem(lax.axis_index("cls"), PAIR))
 
 
 def forward_kernel(
-    shifts, bins, class_ids, defocus, images, right, left, sent, out, pictures, moved, spectra, trig, sems, out_sems
+    shifts_in, bins_in, class_ids_in, defocus_in, images, right_in, left_in, sent,
+    shifts, bins, class_ids, defocus, right, left, out, pictures, moved, spectra, trig,
+    in_sems, sems, out_sems,
 ):
-    def picture_copy(g):
-        part = pl.ds(g * GROUP, GROUP)
-        return pltpu.make_async_copy(images.at[part], pictures.at[part], sems.at[g])
-
-    for g in range(STACK // GROUP):
-        picture_copy(g).start()
+    pairs = [
+        (defocus_in, defocus),
+        (shifts_in, shifts),
+        (bins_in, bins),
+        (class_ids_in, class_ids),
+        (right_in, right),
+        (left_in, left),
+    ]
+    copies = [pltpu.make_async_copy(a, b, in_sems.at[i]) for i, (a, b) in enumerate(pairs)]
+
+    def picture_copy(c):
+        part = pl.ds(c * LOT, LOT)
+        return pltpu.make_async_copy(images.at[part], pictures.at[part], sems.at[c])
+
+    for copy in copies:
+        copy.start()
+    for c in range(STACK // LOT):
+        picture_copy(c).start()
+    for copy in copies[:4]:
+        copy.wait()
 
     lane = lax.broadcasted_iota(jnp.int32, (SIDE, SIDE), 1)
     line = lax.broadcasted_iota(jnp.int32, (SIDE, SIDE), 0)
@@ -115,8 +138,12 @@
     for m in range(TEAM):
         out[m, BLOCK:, :] = tile
 
+    for copy in copies[4:]:
+        copy.wait()
+
     def group(g, carry):
-        picture_copy(g).wait()
+        for c in range(GROUP // LOT):
+            picture_copy(g * (GROUP // LOT) + c).wait()
         shifted = []
         for i in range(GROUP):
             p = g * GROUP + i
@@ -238,14 +265,13 @@
             [average[i * OWNED : (i + 1) * OWNED] for average in averages], axis=0
         )
         for d in range(N_DOM):
-            out[d * PAIR + i] = block
+            out[place(d * PAIR + i)] = block
 
 
 def invert_kernel(arrived, left, right, result, out, rows, sems):
     count = PER * OWNED
-    for q in range(TEAM):
-        m = (q + (LAST - START) * PAIR) % TEAM
-        rows[m * SPREAD : m * SPREAD + count, :] = arrived[q].astype(jnp.float32)
+    for m in range(TEAM):
+        rows[m * SPREAD : m * SPREAD + count, :] = arrived[m].astype(jnp.float32)
 
     def picture(k):
         parts = [rows[pl.ds(j * OWNED + k, TEAM, stride=SPREAD), :] for j in range(PER)]
@@ -278,13 +304,10 @@
         result_copy(k).wait()
 
 
-def teams(start):
-    return [
-        [(d + start) % N_DOM * N_CLS + t * PAIR + i for d in range(N_DOM) for i in range(PAIR)]
-        for t in range(FAR)
-    ]
-
-
+TEAMS = [
+    [m // PAIR * N_CLS + t * PAIR + m % PAIR for m in sorted(range(TEAM), key=place)]
+    for t in range(FAR)
+]
 LINES = [[i + PAIR * t for t in ORDER] for i in range(PAIR)]
 
 
@@ -321,21 +344,28 @@
     payload = pl.pallas_call(
         forward_kernel,
         out_shape=jax.ShapeDtypeStruct((TEAM, BLOCK + TAGS, SIDE), jnp.bfloat16),
-        in_specs=[SMEM, SMEM, SMEM, SMEM, HBM, VMEM, VMEM],
+        in_specs=[HBM] * 7,
         out_specs=HBM,
         scratch_shapes=[
+            pltpu.SMEM((2, STACK), jnp.int32),
+            pltpu.SMEM((STACK,), jnp.int32),
+            pltpu.SMEM((STACK,), jnp.int32),
+            pltpu.SMEM((BINS,), jnp.float32),
+            pltpu.VMEM((SIDE, 2 * SIDE), jnp.bfloat16),
+            pltpu.VMEM((SIDE, 2 * SIDE), jnp.bfloat16),
             pltpu.VMEM((TEAM, BLOCK + TAGS, SIDE), jnp.bfloat16),
             pltpu.VMEM((STACK, SIDE, SIDE), jnp.bfloat16),
             pltpu.VMEM((GROUP, SIDE + 2 * REACH, SIDE), jnp.float32),
             pltpu.VMEM(((STACK + 1) * APART, SIDE), jnp.float32),
             pltpu.VMEM((2, SIDE + BINS, SIDE), jnp.float32),
-            pltpu.SemaphoreType.DMA((STACK // GROUP,)),
+            pltpu.SemaphoreType.DMA((6,)),
+            pltpu.SemaphoreType.DMA((STACK // LOT,)),
             pltpu.SemaphoreType.DMA((TEAM // SLAB,)),
         ],
         compiler_params=ALL,
     )(shifts.T, defocus_bins, class_ids, defocus, images, jnp.asarray(right), jnp.asarray(left))
 
-    arrived = exchange(payload, ("dom", "cls"), teams(START))
+    arrived = exchange(payload, ("dom", "cls"), TEAMS)
     sums = pl.pallas_call(
         gather_kernel,
         out_shape=jax.ShapeDtypeStruct((FAR, PER * NEAR + OWNED, SIDE), jnp.bfloat16),
@@ -353,7 +383,7 @@
         compiler_params=PARAMS,
     )(arrived, squares, own_regular)
 
-    arrived = exchange(averages, ("dom", "cls"), teams(LAST))
+    arrived = exchange(averages, ("dom", "cls"), TEAMS)
     left, right, _ = inverse_tables()
     return pl.pallas_call(
         invert_kernel,

time: 76.3 us -> 75.2 us (0.986)
  no operation moved by 1% of the time
where the time goes in v6:
time: 75.2 us; the launch traced here: 74.9 us
  starting transfers between devices  27.2 us (36%)
  waiting for transfers between devices  21.5 us (29%)
  blocking collectives  16.8 us (22%)
  Pallas kernels  7.92 us (11%)
  local copies, waits for them, and re-layouts  0.85 us (1%)
    all_to_all x2, starting transfers between devices, exchange(): lax.all_to_all(array, axes, split_axis=0, concat_axis=0, tiled=True, axis...  27.2 us
    all_to_all x2, waiting for transfers between devices, exchange(): lax.all_to_all(array, axes, split_axis=0, concat_axis=0, tiled=True, axis...  21.5 us
    all_to_all x1, blocking collectives, exchange(): lax.all_to_all(array, axes, split_axis=0, concat_axis=0, tiled=True, axis...  16.8 us
    pallas_call x1, Pallas kernels, body(): pl.pallas_call(forward_kernel, out_shape=jax.ShapeDtypeStruct((TEAM, BLOC...  4.33 us
    pallas_call x1, Pallas kernels, body(): pl.pallas_call(invert_kernel, out_shape=jax.ShapeDtypeStruct((OWNED, SIDE...  1.89 us
  transfers between devices with their start and end apart: 2, of which 2 were waited for; matrix products, arithmetic and copies ran while one was open for 2% of the time, Pallas kernels for 0%

profile of v6, /device:TPU:1, one launch (start us, length us, event | category | flops | bytes accessed | tf_op | source)
XLA Modules:
  0.0 74.9 jit_solution(9466520323190107556)
XLA Ops:
  0.0 0.0 copy-start
  0.0 4.3 %shard_map.109 = bf16[64,72,128]{2,1,0:T(8,128)(2,1)} custom-call(s32[2,32]{1,0:T(2,128)} %bitcast.26, s32[32]{0:T(128)} %bins_in.1, s32[32]{0:T(128)} %class_ids_in.1, f32[32]{0:T(128)} %defocus_in.1, bf16[32,128,128]{2,1,0:T(8,128)(2,1)} %images.1, bf16[128,256]{1,0:T(8,128)(2,1)} %constant.60.clone.right_in, bf16[128,256]{1,0:T(8,128)(2,1)} %constant.61.clone.left_in), custom_call_target="tpu_custom_call" | custom-call | tf_op jit(solution)/shard_map/pallas_call | solution.py:344
  4.3 0.0 copy-start.3
  4.4 0.0 copy-start.4
  4.4 0.0 copy-start.5
  4.4 14.4 %all-to-all-start = ((bf16[64,72,128]{2,1,0:T(8,128)(2,1)}), bf16[64,72,128]{2,1,0:T(8,128)(2,1)S(1)}, u32[]{:S(2)}, u32[]{:S(2)}) async-start(bf16[64,72,128]{2,1,0:T(8,128)(2,1)} %shard_map.109), calls=%async_computation | async-start | bytes 2359296 | tf_op jit(solution)/shard_map/all_to_all | solution.py:315
  18.8 0.0 copy-done.3
  18.8 0.0 copy-done.4
  18.8 0.1 multiply_add_fusion
  18.9 0.2 dynamic-slice_sine_fusion
  19.1 0.3 copy.22
  19.4 0.3 copy.21
  19.7 0.0 copy-done.5
  19.7 0.1 multiply_cosine_fusion
  19.9 13.3 %all-to-all-done.arrived = bf16[64,72,128]{2,1,0:T(8,128)(2,1)S(1)} async-done(((bf16[64,72,128]{2,1,0:T(8,128)(2,1)}), bf16[64,72,128]{2,1,0:T(8,128)(2,1)S(1)}, u32[]{:S(2)}, u32[]{:S(2)}) %all-to-all-start) | async-done | bytes 1179680 | tf_op jit(solution)/shard_map/all_to_all | solution.py:315
  33.1 1.4 %shard_map.110 = bf16[8,80,128]{2,1,0:T(8,128)(2,1)} custom-call(bf16[64,72,128]{2,1,0:T(8,128)(2,1)S(1)} %all-to-all-done.arrived), custom_call_target="tpu_custom_call" | custom-call | tf_op jit(solution)/shard_map/pallas_call | solution.py:369
  34.5 12.9 %all-to-all-start.1 = ((bf16[8,80,128]{2,1,0:T(8,128)(2,1)}), bf16[8,80,128]{2,1,0:T(8,128)(2,1)S(1)}, u32[]{:S(2)}, u32[]{:S(2)}) async-start(bf16[8,80,128]{2,1,0:T(8,128)(2,1)} %shard_map.110), calls=%async_computation.1 | async-start | bytes 327680 | tf_op jit(solution)/shard_map/all_to_all | solution.py:315
  47.4 0.1 add_multiply_fusion
  47.5 0.0 copy-done
  47.6 8.3 %all-to-all-done.1.arrived = bf16[8,80,128]{2,1,0:T(8,128)(2,1)S(1)} async-done(((bf16[8,80,128]{2,1,0:T(8,128)(2,1)}), bf16[8,80,128]{2,1,0:T(8,128)(2,1)S(1)}, u32[]{:S(2)}, u32[]{:S(2)}) %all-to-all-start.1) | async-done | bytes 163872 | tf_op jit(solution)/shard_map/all_to_all | solution.py:315
  55.9 0.3 shard_map.111
  56.2 16.8 %all_to_all.15.arrived = bf16[64,32,128]{2,1,0:T(8,128)(2,1)S(1)} all-to-all(bf16[64,32,128]{2,1,0:T(8,128)(2,1)S(1)} %shard_map.111), channel_id=1, replica_groups={{336,369,416,449,17,496,97,64,224,257,144,177,417,384,337,304,145,112,2..., dimensions={0} | all-to-all | bytes 1048576 | tf_op jit(solution)/shard_map/all_to_all | solution.py:315
  73.0 0.0 copy-done.1
  73.0 1.9 %shard_map.112 = f32[16,128,128]{2,1,0:T(8,128)} custom-call(bf16[64,32,128]{2,1,0:T(8,128)(2,1)S(1)} %all_to_all.15.arrived, bf16[256,256]{1,0:T(8,128)(2,1)S(1)} %copy-done.1, bf16[256,128]{1,0:T(8,128)(2,1)S(1)} %copy-done.2), custom_call_target="tpu_custom_call" | custom-call | tf_op jit(solution)/shard_map/pallas_call | solution.py:388
  (7 shorter events, 0.0 us)
Async XLA Ops:
  0.0 47.5 %copy-start = (f32[128,128]{1,0:T(8,128)S(1)}, f32[128,128]{1,0:T(8,128)}, u32[]{:S(2)}) copy-start(f32[128,128]{1,0:T(8,128)} %param.16) | copy-start | bytes 196612
  4.3 14.5 %copy-start.3 = (f32[32]{0:T(128)S(1)}, f32[32]{0:T(128)}, u32[]{:S(2)}) copy-start(f32[32]{0:T(128)} %defocus_in.1) | copy-start | bytes 388
  4.4 14.5 %copy-start.4 = (f32[2,64]{1,0:T(2,128)S(1)}, f32[2,64]{1,0:T(2,128)}, u32[]{:S(2)}) copy-start(f32[2,64]{1,0:T(2,128)} %constant.68) | copy-start | bytes 1540
  4.4 15.3 %copy-start.5 = (f32[128]{0:T(128)S(1)}, f32[128]{0:T(128)}, u32[]{:S(2)}) copy-start(f32[128]{0:T(128)} %constant.59.clone) | copy-start | bytes 1540
  4.4 28.8 %all-to-all-start = ((bf16[64,72,128]{2,1,0:T(8,128)(2,1)}), bf16[64,72,128]{2,1,0:T(8,128)(2,1)S(1)}, u32[]{:S(2)}, u32[]{:S(2)}) async-start(bf16[64,72,128]{2,1,0:T(8,128)(2,1)} %shard_map.109), calls=%async_computation | async-start | bytes 2359296 | tf_op jit(solution)/shard_map/all_to_all | solution.py:315
  34.5 38.5 %copy-start.1 = (bf16[256,256]{1,0:T(8,128)(2,1)S(1)}, bf16[256,256]{1,0:T(8,128)(2,1)}, u32[]{:S(2)}) copy-start(bf16[256,256]{1,0:T(8,128)(2,1)} %constant.62.clone.left) | copy-start | bytes 393220
  34.5 38.5 %copy-start.2 = (bf16[256,128]{1,0:T(8,128)(2,1)S(1)}, bf16[256,128]{1,0:T(8,128)(2,1)}, u32[]{:S(2)}) copy-start(bf16[256,128]{1,0:T(8,128)(2,1)} %constant.63.clone.right) | copy-start | bytes 196612
  34.5 21.3 %all-to-all-start.1 = ((bf16[8,80,128]{2,1,0:T(8,128)(2,1)}), bf16[8,80,128]{2,1,0:T(8,128)(2,1)S(1)}, u32[]{:S(2)}, u32[]{:S(2)}) async-start(bf16[8,80,128]{2,1,0:T(8,128)(2,1)} %shard_map.110), calls=%async_computation.1 | async-start | bytes 327680 | tf_op jit(solution)/shard_map/all_to_all | solution.py:315

commit v7 on v6

--- a/solution.py
+++ b/solution.py
@@ -24,6 +24,7 @@
 PER = SIDE // TEAM
 BLOCK = PER * STACK
 TAGS = 8
+LANES = SIDE // BINS
 ORDER = (5, 1, 6, 2, 7, 3, 0, 4)
 STRIDE = 13
 FOLD = 4
@@ -218,11 +219,11 @@
         (((1,), (1,)), ((), ())),
         preferred_element_type=jnp.float32,
     )
-    counts = counts.reshape(FAR, PAIR, OWNED, SIDE)
-    lanes = lax.broadcasted_iota(jnp.int32, (FAR, OWNED, SIDE), 2)
-    counts = jnp.where(lanes < SIDE // 2, counts[:, 0], counts[:, 1])
-    high = jnp.floor(counts * (1.0 / 32.0))
-    digits = jnp.where(lanes % (2 * BINS) < BINS, counts - 32.0 * high, high)
+    counts = counts.reshape(FAR, LANES, TAGS, SIDE)
+    lot = lax.broadcasted_iota(jnp.int32, (FAR, TAGS, SIDE), 2) // BINS
+    digits = counts[:, 0]
+    for i in range(1, LANES):
+        digits = jnp.where(lot == i, counts[:, i], digits)
     sums = sums.astype(jnp.bfloat16)
     digits = digits.astype(jnp.bfloat16)
     for t in range(FAR):
@@ -238,18 +239,14 @@
     total = arrived[0].astype(jnp.float32)
     for z in range(1, FAR):
         total += arrived[z].astype(jnp.float32)
-    lanes = lax.broadcasted_iota(jnp.int32, (OWNED, SIDE), 1)
-    even = lanes % (2 * BINS) < BINS
-    digits = total[PER * NEAR :]
-    ahead = pltpu.roll(digits, SIDE - BINS, axis=1)
-    behind = pltpu.roll(digits, BINS, axis=1)
-    counts = jnp.where(even, digits + 32.0 * ahead, behind + 32.0 * digits)
-    other = pltpu.roll(counts, SIDE // 2, axis=1)
-    near = lanes < SIDE // 2
-    counts = jnp.concatenate(
-        [jnp.where(near, counts, other), jnp.where(near, other, counts)], axis=0
-    )
-    even = jnp.concatenate([even, even], axis=0)
+    lot = lax.broadcasted_iota(jnp.int32, (TAGS, SIDE), 1) // BINS
+    parts = []
+    for i in range(LANES):
+        part = jnp.where(lot == i, total[PER * NEAR :], 0.0)
+        part = part + pltpu.roll(part, SIDE // 2, axis=1)
+        parts.append(part + pltpu.roll(part, BINS, axis=1))
+    counts = jnp.concatenate(parts, axis=0)
+    even = lax.broadcasted_iota(jnp.int32, (NEAR, SIDE), 1) % (2 * BINS) < BINS
     high = jnp.floor(counts * (1.0 / 128.0))
     digits = jnp.where(even, counts - 128.0 * high, high).astype(jnp.bfloat16)
     denominator = jnp.dot(digits, squares[...], preferred_element_type=jnp.float32)
@@ -368,7 +365,7 @@
     arrived = exchange(payload, ("dom", "cls"), TEAMS)
     sums = pl.pallas_call(
         gather_kernel,
-        out_shape=jax.ShapeDtypeStruct((FAR, PER * NEAR + OWNED, SIDE), jnp.bfloat16),
+        out_shape=jax.ShapeDtypeStruct((FAR, PER * NEAR + TAGS, SIDE), jnp.bfloat16),
         in_specs=[VMEM],
         out_specs=VMEM,
         compiler_params=PARAMS,

time: 75.2 us -> 74.5 us (level)
  no operation moved by 1% of the time
where the time goes in v7:
time: 74.5 us; the launch traced here: 74.2 us
  starting transfers between devices  27.2 us (37%)
  waiting for transfers between devices  21.2 us (28%)
  blocking collectives  16.4 us (22%)
  Pallas kernels  7.92 us (11%)
  local copies, waits for them, and re-layouts  0.85 us (1%)
    all_to_all x2, starting transfers between devices, exchange(): lax.all_to_all(array, axes, split_axis=0, concat_axis=0, tiled=True, axis...  27.2 us
    all_to_all x2, waiting for transfers between devices, exchange(): lax.all_to_all(array, axes, split_axis=0, concat_axis=0, tiled=True, axis...  21.2 us
    all_to_all x1, blocking collectives, exchange(): lax.all_to_all(array, axes, split_axis=0, concat_axis=0, tiled=True, axis...  16.4 us
    pallas_call x1, Pallas kernels, body(): pl.pallas_call(forward_kernel, out_shape=jax.ShapeDtypeStruct((TEAM, BLOC...  4.34 us
    pallas_call x1, Pallas kernels, body(): pl.pallas_call(invert_kernel, out_shape=jax.ShapeDtypeStruct((OWNED, SIDE...  1.89 us
  transfers between devices with their start and end apart: 2, of which 2 were waited for; matrix products, arithmetic and copies ran while one was open for 2% of the time, Pallas kernels for 0%

profile of v7, /device:TPU:1, one launch (start us, length us, event | category | flops | bytes accessed | tf_op | source)
XLA Modules:
  0.0 74.2 jit_solution(17682006719153665470)
XLA Ops:
  0.0 0.0 copy-start
  0.0 4.3 %shard_map.109 = bf16[64,72,128]{2,1,0:T(8,128)(2,1)} custom-call(s32[2,32]{1,0:T(2,128)} %bitcast.26, s32[32]{0:T(128)} %bins_in.1, s32[32]{0:T(128)} %class_ids_in.1, f32[32]{0:T(128)} %defocus_in.1, bf16[32,128,128]{2,1,0:T(8,128)(2,1)} %images.1, bf16[128,256]{1,0:T(8,128)(2,1)} %constant.60.clone.right_in, bf16[128,256]{1,0:T(8,128)(2,1)} %constant.61.clone.left_in), custom_call_target="tpu_custom_call" | custom-call | tf_op jit(solution)/shard_map/pallas_call | solution.py:341
  4.3 0.0 copy-start.3
  4.4 0.0 copy-start.4
  4.4 0.0 copy-start.5
  4.4 14.4 %all-to-all-start = ((bf16[64,72,128]{2,1,0:T(8,128)(2,1)}), bf16[64,72,128]{2,1,0:T(8,128)(2,1)S(1)}, u32[]{:S(2)}, u32[]{:S(2)}) async-start(bf16[64,72,128]{2,1,0:T(8,128)(2,1)} %shard_map.109), calls=%async_computation | async-start | bytes 2359296 | tf_op jit(solution)/shard_map/all_to_all | solution.py:312
  18.8 0.0 copy-done.3
  18.8 0.0 copy-done.4
  18.8 0.1 multiply_add_fusion
  18.9 0.2 dynamic-slice_sine_fusion
  19.1 0.3 copy.22
  19.4 0.3 copy.21
  19.7 0.0 copy-done.5
  19.7 0.1 multiply_cosine_fusion
  19.9 13.3 %all-to-all-done.arrived = bf16[64,72,128]{2,1,0:T(8,128)(2,1)S(1)} async-done(((bf16[64,72,128]{2,1,0:T(8,128)(2,1)}), bf16[64,72,128]{2,1,0:T(8,128)(2,1)S(1)}, u32[]{:S(2)}, u32[]{:S(2)}) %all-to-all-start) | async-done | bytes 1179680 | tf_op jit(solution)/shard_map/all_to_all | solution.py:312
  33.1 1.4 %shard_map.110 = bf16[8,72,128]{2,1,0:T(8,128)(2,1)} custom-call(bf16[64,72,128]{2,1,0:T(8,128)(2,1)S(1)} %all-to-all-done.arrived), custom_call_target="tpu_custom_call" | custom-call | tf_op jit(solution)/shard_map/pallas_call | solution.py:366
  34.5 12.9 %all-to-all-start.1 = ((bf16[8,72,128]{2,1,0:T(8,128)(2,1)}), bf16[8,72,128]{2,1,0:T(8,128)(2,1)S(1)}, u32[]{:S(2)}, u32[]{:S(2)}) async-start(bf16[8,72,128]{2,1,0:T(8,128)(2,1)} %shard_map.110), calls=%async_computation.1 | async-start | bytes 294912 | tf_op jit(solution)/shard_map/all_to_all | solution.py:312
  47.4 0.1 add_multiply_fusion
  47.5 0.0 copy-done
  47.6 7.9 %all-to-all-done.1.arrived = bf16[8,72,128]{2,1,0:T(8,128)(2,1)S(1)} async-done(((bf16[8,72,128]{2,1,0:T(8,128)(2,1)}), bf16[8,72,128]{2,1,0:T(8,128)(2,1)S(1)}, u32[]{:S(2)}, u32[]{:S(2)}) %all-to-all-start.1) | async-done | bytes 147488 | tf_op jit(solution)/shard_map/all_to_all | solution.py:312
  55.5 0.3 shard_map.111
  55.9 16.4 %all_to_all.15.arrived = bf16[64,32,128]{2,1,0:T(8,128)(2,1)S(1)} all-to-all(bf16[64,32,128]{2,1,0:T(8,128)(2,1)S(1)} %shard_map.111), channel_id=1, replica_groups={{336,369,416,449,17,496,97,64,224,257,144,177,417,384,337,304,145,112,2..., dimensions={0} | all-to-all | bytes 1048576 | tf_op jit(solution)/shard_map/all_to_all | solution.py:312
  72.3 0.0 copy-done.1
  72.3 1.9 %shard_map.112 = f32[16,128,128]{2,1,0:T(8,128)} custom-call(bf16[64,32,128]{2,1,0:T(8,128)(2,1)S(1)} %all_to_all.15.arrived, bf16[256,256]{1,0:T(8,128)(2,1)S(1)} %copy-done.1, bf16[256,128]{1,0:T(8,128)(2,1)S(1)} %copy-done.2), custom_call_target="tpu_custom_call" | custom-call | tf_op jit(solution)/shard_map/pallas_call | solution.py:385
  (7 shorter events, 0.0 us)
Async XLA Ops:
  0.0 47.5 %copy-start = (f32[128,128]{1,0:T(8,128)S(1)}, f32[128,128]{1,0:T(8,128)}, u32[]{:S(2)}) copy-start(f32[128,128]{1,0:T(8,128)} %param.16) | copy-start | bytes 196612
  4.3 14.5 %copy-start.3 = (f32[32]{0:T(128)S(1)}, f32[32]{0:T(128)}, u32[]{:S(2)}) copy-start(f32[32]{0:T(128)} %defocus_in.1) | copy-start | bytes 388
  4.4 14.5 %copy-start.4 = (f32[2,64]{1,0:T(2,128)S(1)}, f32[2,64]{1,0:T(2,128)}, u32[]{:S(2)}) copy-start(f32[2,64]{1,0:T(2,128)} %constant.68) | copy-start | bytes 1540
  4.4 15.3 %copy-start.5 = (f32[128]{0:T(128)S(1)}, f32[128]{0:T(128)}, u32[]{:S(2)}) copy-start(f32[128]{0:T(128)} %constant.59.clone) | copy-start | bytes 1540
  4.4 28.7 %all-to-all-start = ((bf16[64,72,128]{2,1,0:T(8,128)(2,1)}), bf16[64,72,128]{2,1,0:T(8,128)(2,1)S(1)}, u32[]{:S(2)}, u32[]{:S(2)}) async-start(bf16[64,72,128]{2,1,0:T(8,128)(2,1)} %shard_map.109), calls=%async_computation | async-start | bytes 2359296 | tf_op jit(solution)/shard_map/all_to_all | solution.py:312
  34.5 37.8 %copy-start.1 = (bf16[256,256]{1,0:T(8,128)(2,1)S(1)}, bf16[256,256]{1,0:T(8,128)(2,1)}, u32[]{:S(2)}) copy-start(bf16[256,256]{1,0:T(8,128)(2,1)} %constant.62.clone.left) | copy-start | bytes 393220
  34.5 37.8 %copy-start.2 = (bf16[256,128]{1,0:T(8,128)(2,1)S(1)}, bf16[256,128]{1,0:T(8,128)(2,1)}, u32[]{:S(2)}) copy-start(bf16[256,128]{1,0:T(8,128)(2,1)} %constant.63.clone.right) | copy-start | bytes 196612
  34.5 21.0 %all-to-all-start.1 = ((bf16[8,72,128]{2,1,0:T(8,128)(2,1)}), bf16[8,72,128]{2,1,0:T(8,128)(2,1)S(1)}, u32[]{:S(2)}, u32[]{:S(2)}) async-start(bf16[8,72,128]{2,1,0:T(8,128)(2,1)} %shard_map.110), calls=%async_computation.1 | async-start | bytes 294912 | tf_op jit(solution)/shard_map/all_to_all | solution.py:312

commit v8 on v7

--- a/solution.py
+++ b/solution.py
@@ -102,9 +102,13 @@
         part = pl.ds(c * LOT, LOT)
         return pltpu.make_async_copy(images.at[part], pictures.at[part], sems.at[c])
 
-    for copy in copies:
+    for copy in copies[:4]:
         copy.start()
-    for c in range(STACK // LOT):
+    for c in range(GROUP // LOT):
+        picture_copy(c).start()
+    for copy in copies[4:]:
+        copy.start()
+    for c in range(GROUP // LOT, STACK // LOT):
         picture_copy(c).start()
     for copy in copies[:4]:
         copy.wait()

time: 74.5 us -> 74.5 us (level)
  no operation moved by 1% of the time
where the time goes in v8:
time: 74.5 us; the launch traced here: 74.2 us
  starting transfers between devices  27.2 us (37%)
  waiting for transfers between devices  21.2 us (28%)
  blocking collectives  16.4 us (22%)
  Pallas kernels  7.92 us (11%)
  local copies, waits for them, and re-layouts  0.85 us (1%)
    all_to_all x2, starting transfers between devices, exchange(): lax.all_to_all(array, axes, split_axis=0, concat_axis=0, tiled=True, axis...  27.2 us
    all_to_all x2, waiting for transfers between devices, exchange(): lax.all_to_all(array, axes, split_axis=0, concat_axis=0, tiled=True, axis...  21.2 us
    all_to_all x1, blocking collectives, exchange(): lax.all_to_all(array, axes, split_axis=0, concat_axis=0, tiled=True, axis...  16.4 us
    pallas_call x1, Pallas kernels, body(): pl.pallas_call(forward_kernel, out_shape=jax.ShapeDtypeStruct((TEAM, BLOC...  4.34 us
    pallas_call x1, Pallas kernels, body(): pl.pallas_call(invert_kernel, out_shape=jax.ShapeDtypeStruct((OWNED, SIDE...  1.89 us
  transfers between devices with their start and end apart: 2, of which 2 were waited for; matrix products, arithmetic and copies ran while one was open for 2% of the time, Pallas kernels for 0%

profile of v8, /device:TPU:1, one launch (start us, length us, event | category | flops | bytes accessed | tf_op | source)
XLA Modules:
  0.0 74.2 jit_solution(17682006719153665470)
XLA Ops:
  0.0 0.0 copy-start
  0.0 4.3 %shard_map.109 = bf16[64,72,128]{2,1,0:T(8,128)(2,1)} custom-call(s32[2,32]{1,0:T(2,128)} %bitcast.26, s32[32]{0:T(128)} %bins_in.1, s32[32]{0:T(128)} %class_ids_in.1, f32[32]{0:T(128)} %defocus_in.1, bf16[32,128,128]{2,1,0:T(8,128)(2,1)} %images.1, bf16[128,256]{1,0:T(8,128)(2,1)} %constant.60.clone.right_in, bf16[128,256]{1,0:T(8,128)(2,1)} %constant.61.clone.left_in), custom_call_target="tpu_custom_call" | custom-call | tf_op jit(solution)/shard_map/pallas_call | solution.py:345
  4.3 0.0 copy-start.3
  4.4 0.0 copy-start.4
  4.4 0.0 copy-start.5
  4.4 14.4 %all-to-all-start = ((bf16[64,72,128]{2,1,0:T(8,128)(2,1)}), bf16[64,72,128]{2,1,0:T(8,128)(2,1)S(1)}, u32[]{:S(2)}, u32[]{:S(2)}) async-start(bf16[64,72,128]{2,1,0:T(8,128)(2,1)} %shard_map.109), calls=%async_computation | async-start | bytes 2359296 | tf_op jit(solution)/shard_map/all_to_all | solution.py:316
  18.8 0.0 copy-done.3
  18.8 0.0 copy-done.4
  18.8 0.1 multiply_add_fusion
  18.9 0.2 dynamic-slice_sine_fusion
  19.1 0.3 copy.22
  19.4 0.3 copy.21
  19.7 0.0 copy-done.5
  19.7 0.1 multiply_cosine_fusion
  19.8 13.3 %all-to-all-done.arrived = bf16[64,72,128]{2,1,0:T(8,128)(2,1)S(1)} async-done(((bf16[64,72,128]{2,1,0:T(8,128)(2,1)}), bf16[64,72,128]{2,1,0:T(8,128)(2,1)S(1)}, u32[]{:S(2)}, u32[]{:S(2)}) %all-to-all-start) | async-done | bytes 1179680 | tf_op jit(solution)/shard_map/all_to_all | solution.py:316
  33.1 1.4 %shard_map.110 = bf16[8,72,128]{2,1,0:T(8,128)(2,1)} custom-call(bf16[64,72,128]{2,1,0:T(8,128)(2,1)S(1)} %all-to-all-done.arrived), custom_call_target="tpu_custom_call" | custom-call | tf_op jit(solution)/shard_map/pallas_call | solution.py:370
  34.5 12.9 %all-to-all-start.1 = ((bf16[8,72,128]{2,1,0:T(8,128)(2,1)}), bf16[8,72,128]{2,1,0:T(8,128)(2,1)S(1)}, u32[]{:S(2)}, u32[]{:S(2)}) async-start(bf16[8,72,128]{2,1,0:T(8,128)(2,1)} %shard_map.110), calls=%async_computation.1 | async-start | bytes 294912 | tf_op jit(solution)/shard_map/all_to_all | solution.py:316
  47.4 0.1 add_multiply_fusion
  47.5 0.0 copy-done
  47.6 7.9 %all-to-all-done.1.arrived = bf16[8,72,128]{2,1,0:T(8,128)(2,1)S(1)} async-done(((bf16[8,72,128]{2,1,0:T(8,128)(2,1)}), bf16[8,72,128]{2,1,0:T(8,128)(2,1)S(1)}, u32[]{:S(2)}, u32[]{:S(2)}) %all-to-all-start.1) | async-done | bytes 147488 | tf_op jit(solution)/shard_map/all_to_all | solution.py:316
  55.5 0.3 shard_map.111
  55.9 16.4 %all_to_all.15.arrived = bf16[64,32,128]{2,1,0:T(8,128)(2,1)S(1)} all-to-all(bf16[64,32,128]{2,1,0:T(8,128)(2,1)S(1)} %shard_map.111), channel_id=1, replica_groups={{336,369,416,449,17,496,97,64,224,257,144,177,417,384,337,304,145,112,2..., dimensions={0} | all-to-all | bytes 1048576 | tf_op jit(solution)/shard_map/all_to_all | solution.py:316
  72.3 0.0 copy-done.1
  72.3 1.9 %shard_map.112 = f32[16,128,128]{2,1,0:T(8,128)} custom-call(bf16[64,32,128]{2,1,0:T(8,128)(2,1)S(1)} %all_to_all.15.arrived, bf16[256,256]{1,0:T(8,128)(2,1)S(1)} %copy-done.1, bf16[256,128]{1,0:T(8,128)(2,1)S(1)} %copy-done.2), custom_call_target="tpu_custom_call" | custom-call | tf_op jit(solution)/shard_map/pallas_call | solution.py:389
  (7 shorter events, 0.0 us)
Async XLA Ops:
  0.0 47.5 %copy-start = (f32[128,128]{1,0:T(8,128)S(1)}, f32[128,128]{1,0:T(8,128)}, u32[]{:S(2)}) copy-start(f32[128,128]{1,0:T(8,128)} %param.16) | copy-start | bytes 196612
  4.3 14.4 %copy-start.3 = (f32[32]{0:T(128)S(1)}, f32[32]{0:T(128)}, u32[]{:S(2)}) copy-start(f32[32]{0:T(128)} %defocus_in.1) | copy-start | bytes 388
  4.4 14.4 %copy-start.4 = (f32[2,64]{1,0:T(2,128)S(1)}, f32[2,64]{1,0:T(2,128)}, u32[]{:S(2)}) copy-start(f32[2,64]{1,0:T(2,128)} %constant.68) | copy-start | bytes 1540
  4.4 15.3 %copy-start.5 = (f32[128]{0:T(128)S(1)}, f32[128]{0:T(128)}, u32[]{:S(2)}) copy-start(f32[128]{0:T(128)} %constant.59.clone) | copy-start | bytes 1540
  4.4 28.7 %all-to-all-start = ((bf16[64,72,128]{2,1,0:T(8,128)(2,1)}), bf16[64,72,128]{2,1,0:T(8,128)(2,1)S(1)}, u32[]{:S(2)}, u32[]{:S(2)}) async-start(bf16[64,72,128]{2,1,0:T(8,128)(2,1)} %shard_map.109), calls=%async_computation | async-start | bytes 2359296 | tf_op jit(solution)/shard_map/all_to_all | solution.py:316
  34.5 37.8 %copy-start.1 = (bf16[256,256]{1,0:T(8,128)(2,1)S(1)}, bf16[256,256]{1,0:T(8,128)(2,1)}, u32[]{:S(2)}) copy-start(bf16[256,256]{1,0:T(8,128)(2,1)} %constant.62.clone.left) | copy-start | bytes 393220
  34.5 37.8 %copy-start.2 = (bf16[256,128]{1,0:T(8,128)(2,1)S(1)}, bf16[256,128]{1,0:T(8,128)(2,1)}, u32[]{:S(2)}) copy-start(bf16[256,128]{1,0:T(8,128)(2,1)} %constant.63.clone.right) | copy-start | bytes 196612
  34.5 21.0 %all-to-all-start.1 = ((bf16[8,72,128]{2,1,0:T(8,128)(2,1)}), bf16[8,72,128]{2,1,0:T(8,128)(2,1)S(1)}, u32[]{:S(2)}, u32[]{:S(2)}) async-start(bf16[8,72,128]{2,1,0:T(8,128)(2,1)} %shard_map.110), calls=%async_computation.1 | async-start | bytes 294912 | tf_op jit(solution)/shard_map/all_to_all | solution.py:316
